TPU v7x, 256 devices: a whole 4x4x8 slice. The times are simulated.
256 devices in a mesh: sub: 4 (over y_lo, core), prow: 8 (over z), pcol: 8 (over y_hi, x).
Axes of the slice: x: 4, y: 4 (y_hi: 2, y_lo: 2; y = y_hi * 2 + y_lo), z: 8, core: 2. Of those that a mesh axis runs over, the one named last changes fastest.
Arguments:
- child_front: float32 [4, 6656, 6656], P('sub', 'prow', 'pcol')
- child_order: int32 [4, 512], P('sub'), may hold values from 0 to 511, as said below
- parent_front: float32 [8704, 8704], P('prow', ('sub', 'pcol'))
- parent_order: int32 [512], replicated, may hold values from 0 to 511, as said below
- row_map: int32 [4, 48], P('sub', 'prow'), may hold values from 0 to 63, as said below
- col_map: int32 [4, 48], P('sub', 'pcol'), may hold values from 0 to 63, as said below
Outputs:
- child_lower: float32 [4, 6144, 512], P('sub', 'prow', 'pcol')
- parent_lower: float32 [8192, 512], P('prow', ('sub', 'pcol'))
- parent_schur: float32 [8192, 8192], P('prow', ('sub', 'pcol'))
Inputs may be any that keep to these rules, and one draw needn't show every extreme that they name: `child_order`: each row is a permutation of 0 to 511. `parent_order`: A permutation of 0 to 511. Within one child the values are distinct; trailing row block i of a child, held by process row i // 6, goes to a parent trailing row block held by the same process row, that is row_map[s, i] // 8 == i // 6. Within one child the values are distinct; child trailing column block j, held by process column j // 6, goes to a parent trailing column block held by a parent column device whose pcol index is the same: (col_map[s, j] // 2) % 8 == j // 6.
All inputs are finite; a program needn't handle non-finite values.
Results may differ from a plain program's by a relative error of at most 0.0001.
Values sent between devices are 32-bit elements; how exact they have to be, the bound alone decides.
No kernel may reach another device: no remote copies, remote signals or barrier semaphores. Data moves between devices by JAX's collectives and lax.ppermute only.
A program may use at most 128 MiB of HBM per device.

v0:
```python
import jax
import jax.numpy as jnp
from jax import lax
from jax.sharding import PartitionSpec as P

PB = 512
BLK = 128
NS_STEPS = 5


HIGH = lax.Precision.HIGHEST


def inverse_of(panel_block):
    eye = jnp.eye(panel_block.shape[0], dtype=jnp.float32)
    estimate = jnp.diag(1.0 / jnp.diagonal(panel_block))
    for sweep in range(NS_STEPS):
        inner = 2.0 * eye - jnp.dot(
            panel_block, estimate, precision=HIGH, preferred_element_type=jnp.float32
        )
        estimate = jnp.dot(estimate, inner, precision=HIGH, preferred_element_type=jnp.float32)
    return estimate


def eliminate(panel_block, left_cols, upper_rows, trailing, start, width):
    inverse_est = inverse_of(panel_block)
    lower_part = jnp.dot(left_cols, inverse_est, precision=HIGH, preferred_element_type=jnp.float32)
    own_lower = lax.dynamic_slice_in_dim(lower_part, start, width, 1)
    schur = trailing - jnp.dot(
        lower_part, upper_rows, precision=HIGH, preferred_element_type=jnp.float32
    )
    return (own_lower, schur)


def one_hot(values, count):
    return (values[None, :] == jnp.arange(count, dtype=jnp.int32)[:, None]).astype(jnp.float32)


def place_blocks(rows_hot, piece, cols_hot):
    p_count, j_count = rows_hot.shape
    q_count, k_count = cols_hot.shape
    blocks = piece.reshape(j_count, BLK, k_count, BLK)
    placed = jnp.einsum("pj,jakb,qk->paqb", rows_hot, blocks, cols_hot, precision=HIGH)
    return placed.reshape(p_count * BLK, q_count * BLK)


def body(child_front, child_order, parent_front, parent_order, row_map, col_map):
    rows_n = lax.axis_size("prow")
    cols_n = lax.axis_size("pcol")
    subs_n = lax.axis_size("sub")
    front_block = child_front[0]
    child_rows = PB // rows_n
    child_cols = PB // cols_n
    pieces = lax.all_gather(
        front_block[:child_rows, :child_cols][None], ("prow", "pcol"), axis=0, tiled=True
    )
    panel_block = (
        pieces.reshape(rows_n, cols_n, child_rows, child_cols).transpose(0, 2, 1, 3).reshape(PB, PB)
    )
    upper_rows = lax.all_gather(front_block[:child_rows, child_cols:], "prow", axis=0, tiled=True)
    left_cols = lax.all_gather(front_block[child_rows:, :child_cols], "pcol", axis=1, tiled=True)
    pivot_seq = child_order[0]
    panel_block = panel_block[:, pivot_seq]
    left_cols = left_cols[:, pivot_seq]
    trailing = front_block[child_rows:, child_cols:]
    own_lower, schur = eliminate(
        panel_block,
        left_cols,
        upper_rows,
        trailing,
        lax.axis_index("pcol") * child_cols,
        child_cols,
    )
    parent_piv = PB // (subs_n * cols_n)
    row_blocks = (parent_front.shape[0] - child_rows) // BLK
    col_blocks = (parent_front.shape[1] - parent_piv) // BLK
    col_vals = col_map[0]
    col_target = col_vals // col_blocks // cols_n * col_blocks + col_vals % col_blocks
    placed = place_blocks(
        one_hot(row_map[0] % row_blocks, row_blocks),
        schur,
        one_hot(col_target, subs_n * col_blocks),
    )
    contribution = lax.psum_scatter(placed, "sub", scatter_dimension=1, tiled=True)
    parent_pieces = lax.all_gather(
        parent_front[:child_rows, :parent_piv][None], ("sub", "prow", "pcol"), axis=0, tiled=True
    )
    parent_panel = (
        parent_pieces.reshape(subs_n, rows_n, cols_n, child_rows, parent_piv)
        .transpose(1, 3, 0, 2, 4)
        .reshape(PB, PB)
    )
    parent_upper = lax.all_gather(
        parent_front[:child_rows, parent_piv:], "prow", axis=0, tiled=True
    )
    parent_left = lax.all_gather(
        parent_front[child_rows:, :parent_piv], ("sub", "pcol"), axis=1, tiled=True
    )
    parent_panel = parent_panel[:, parent_order]
    parent_left = parent_left[:, parent_order]
    parent_trail = parent_front[child_rows:, parent_piv:] + contribution
    parent_own, parent_schur = eliminate(
        parent_panel,
        parent_left,
        parent_upper,
        parent_trail,
        lax.axis_index(("sub", "pcol")) * parent_piv,
        parent_piv,
    )
    return (own_lower[None], parent_own, parent_schur)


def solution(mesh):
    placed = (
        P("sub", "prow", "pcol"),
        P("sub", None),
        P("prow", ("sub", "pcol")),
        P(),
        P("sub", "prow"),
        P("sub", "pcol"),
    )
    return jax.shard_map(
        body,
        mesh=mesh,
        in_specs=placed,
        out_specs=(
            P("sub", "prow", "pcol"),
            P("prow", ("sub", "pcol")),
            P("prow", ("sub", "pcol")),
        ),
        check_vma=False,
    )
```

profile of v0, /device:TPU:1, one launch (start us, length us, event | category | flops | bytes accessed | tf_op | source)
XLA Modules:
  0.0 1076.6 jit_solution(17146361914170432118)
XLA Ops:
  7.2 0.0 all-gather.15.cloned.1.call-start
  7.2 1.4 slice.45
  8.6 0.0 all-gather.9.cloned.1.call-start
  8.7 1.0 slice.44
  9.7 0.8 copy.18
  10.6 0.0 all-gather.13.cloned.1.call-start
  10.6 1.7 slice.47
  12.4 0.0 all-gather.17.cloned.1.call-start
  12.4 1.3 slice_bitcast_fusion
  13.8 0.0 all-gather.11.cloned.1.call-start
  13.8 1.6 slice.26
  15.4 0.0 reduce-scatter.2.cloned.1.call-start
  15.6 114.6 %all-gather.15.cloned.1.call-done = f32[4096,64]{1,0:T(8,128)} async-done(((f32[64,64]{1,0:T(8,128)}), f32[4096,64]{1,0:T(8,128)}) %all-gather.15.cloned.1.call-update) | async-done | bytes 1048592 | tf_op jit(solution)/shard_map/all_gather | solution.py:54
  130.2 2.9 copy.19
  133.1 1.9 reshape.59
  135.0 1.6 gather_fusion.1
  136.7 4.8 gather_fusion.2
  141.5 2.0 select_subtract_fusion.9
  143.5 1.8 fusion.13
  145.4 1.9 select_subtract_fusion.8
  147.3 1.9 fusion.41
  149.2 1.9 select_subtract_fusion.7
  151.1 1.8 fusion.42
  152.9 2.5 select_subtract_fusion.6
  155.4 1.8 fusion.43
  157.3 1.9 select_subtract_fusion.5
  159.2 2.8 fusion.44
  162.0 26.4 %all-gather.9.cloned.1.call-done = f32[768,512]{0,1:T(8,128)} async-done(((f32[768,64]{0,1:T(8,128)}), f32[768,512]{0,1:T(8,128)}) %all-gather.9.cloned.1.call-update) | async-done | bytes 1572880 | tf_op jit(solution)/shard_map/all_gather | solution.py:61
  188.4 3.9 gather_fusion
  192.3 4.1 fusion.45
  196.4 30.4 %all-gather.13.cloned.1.call-done = f32[512,768]{1,0:T(8,128)} async-done(((f32[64,768]{1,0:T(8,128)}), f32[512,768]{1,0:T(8,128)}) %all-gather.13.cloned.1.call-update) | async-done | bytes 1572880 | tf_op jit(solution)/shard_map/all_gather | solution.py:60
  226.8 7.5 slice_subtract_fusion
  234.3 2.5 reshape.62
  236.8 2.9 fusion.2
  239.7 2.5 fusion.4
  242.2 0.3 copy.24
  242.5 2.9 copy.39
  245.5 1.3 copy-done.1
  246.7 0.3 slice.28
  247.1 1.3 copy.28
  248.4 0.1 copy.29
  248.5 21.3 %all_gather.23 = f32[512,256]{1,0:T(8,128)} all-gather(f32[64,256]{1,0:T(8,128)S(1)} %copy.29), channel_id=1, replica_groups=mesh['sub'=4,'prow'=8,'pcol'=8] {'prow'}, dimensions={0}, use_global_device_ids=true | all-gather | bytes 589824 | tf_op jit(solution)/shard_map/all_gather | solution.py:93
  269.8 656.2 %all-gather.17.cloned.1.call-done = f32[256,64,16]{1,2,0:T(8,128)} async-done(((f32[1,64,16]{1,2,0:T(8,128)}), f32[256,64,16]{1,2,0:T(8,128)}) %all-gather.17.cloned.1.call-update) | async-done | bytes 1048592 | tf_op jit(solution)/shard_map/all_gather | solution.py:85
  926.1 4.2 copy.40
  930.3 1.9 reshape.61
  932.2 1.6 gather_fusion.4
  933.9 4.8 gather_fusion.5
  938.6 2.0 select_subtract_fusion.4
  940.6 1.8 fusion.7
  942.5 1.9 select_subtract_fusion.3
  944.4 1.8 fusion.46
  946.3 1.9 select_subtract_fusion.2
  948.2 1.8 fusion.47
  950.1 2.3 select_subtract_fusion.1
  952.4 1.8 fusion.48
  954.3 1.9 select_subtract_fusion
  956.2 1.8 fusion.49
  958.0 1.6 dynamic-slice_bitcast_fusion
  959.7 52.7 %all-gather.11.cloned.1.call-done = f32[1024,512]{0,1:T(8,128)} async-done(((f32[1024,16]{0,1:T(8,128)}), f32[1024,512]{0,1:T(8,128)}) %all-gather.11.cloned.1.call-update) | async-done | bytes 2097168 | tf_op jit(solution)/shard_map/all_gather | solution.py:96
  1012.4 5.4 gather_fusion.3
  1017.8 5.1 fusion.50
  1022.9 0.6 constant_dynamic-slice_fusion
  1023.6 39.9 %reduce-scatter.2.cloned.1.call-done = f32[1024,256]{1,0:T(8,128)} async-done(((f32[1024,1024]{1,0:T(8,128)}), f32[1024,256]{1,0:T(8,128)}) %reduce-scatter.2.cloned.1.call-update) | async-done | bytes 1048592 | tf_op jit(solution)/shard_map/reduce_scatter | solution.py:84
  1063.5 6.1 convolution_subtract_fusion
  (27 shorter events, 0.2 us)
Async XLA Ops:
  7.2 8.3 copy-start.2
  7.2 8.4 copy-start.4
  7.2 8.4 copy-start.5
  7.2 123.0 %all-gather.15.cloned.1.call-start = ((), (), s32[]{:S(2)}) async-start(), calls=%async_computation.5 | async-start | bytes 2129920 | tf_op jit(solution)/shard_map/all_gather | solution.py:54
  8.6 179.8 %all-gather.9.cloned.1.call-start = ((), (), s32[]{:S(2)}) async-start(), calls=%async_computation.1 | async-start | bytes 1769472 | tf_op jit(solution)/shard_map/all_gather | solution.py:61
  10.6 216.2 %all-gather.13.cloned.1.call-start = ((), (), s32[]{:S(2)}) async-start(), calls=%async_computation.3 | async-start | bytes 1769472 | tf_op jit(solution)/shard_map/all_gather | solution.py:60
  12.4 913.7 %all-gather.17.cloned.1.call-start = ((), (), s32[]{:S(2)}) async-start(), calls=%async_computation.6 | async-start | bytes 2105344 | tf_op jit(solution)/shard_map/all_gather | solution.py:85
  13.8 998.6 %all-gather.11.cloned.1.call-start = ((), (), s32[]{:S(2)}) async-start(), calls=%async_computation.2 | async-start | bytes 2162688 | tf_op jit(solution)/shard_map/all_gather | solution.py:96
  15.4 1048.1 %reduce-scatter.2.cloned.1.call-start = ((), (), s32[]{:S(2)}) async-start(), calls=%async_computation.4 | async-start | bytes 5242880 | tf_op jit(solution)/shard_map/reduce_scatter | solution.py:84
  196.4 30.4 %copy-start = (f32[768,512]{0,1:T(8,128)}, f32[768,512]{0,1:T(8,128)S(1)}, u32[]{:S(2)}) copy-start(f32[768,512]{0,1:T(8,128)S(1)} %fusion.45) | copy-start | bytes 4718596
  245.4 1.3 copy-start.1
  246.7 1.8 copy-start.3
Sparse Core Ops, SparseCore 0:
  12.2 117.9 all-gather.14
  133.4 54.9 all-gather.8
  190.2 36.5 all-gather.12
  228.5 697.5 all-gather.16
  928.3 84.0 all-gather.10
  1014.8 48.6 reduce-scatter.1
where the time goes:
time: 1080 us
  waiting for transfers between devices  920 us (85%)
  matrix products  68 us (6%)
  local copies, waits for them, and re-layouts  52 us (5%)
  blocking collectives  21.3 us (2%)
  between operations  14.7 us (1%)
    all_gather x1, waiting for transfers between devices, body(): lax.all_gather(parent_front[:child_rows, :parent_piv][None], ('sub', 'pro...  656 us
    all_gather x1, waiting for transfers between devices, body(): lax.all_gather(front_block[:child_rows, :child_cols][None], ('prow', 'pco...  115 us
    all_gather x1, waiting for transfers between devices, body(): lax.all_gather(parent_front[child_rows:, :parent_piv], ('sub', 'pcol'), a...  52.7 us
    reduce_scatter x1, waiting for transfers between devices, body(): lax.psum_scatter(placed, 'sub', scatter_dimension=1, tiled=True)  39.9 us
    all_gather x1, waiting for transfers between devices, body(): lax.all_gather(front_block[:child_rows, child_cols:], 'prow', axis=0, til...  30.4 us
    all_gather x1, waiting for transfers between devices, body(): lax.all_gather(front_block[child_rows:, :child_cols], 'pcol', axis=1, til...  26.4 us
  transfers between devices with their start and end apart: 6, of which 6 were waited for; matrix products, arithmetic and copies ran while one was open for 10% of the time, Pallas kernels for 0%

commit v1 on v0

v1 whole, which is shorter than its diff:
```python
import functools

import jax
import jax.numpy as jnp
from jax import lax
from jax.experimental import pallas as pl
from jax.experimental.pallas import tpu as pltpu
from jax.sharding import PartitionSpec as P

PB = 512
BLK = 128
N = 64
PP = 16
CT = 768
PT = 1024
F32 = jnp.float32
BF16 = jnp.bfloat16
VMEM = pl.BlockSpec(memory_space=pltpu.VMEM)
ANY = pl.BlockSpec(memory_space=pl.ANY)
SMEM = pl.BlockSpec(memory_space=pltpu.SMEM)


def flip(axis, size, mask):
    return functools.partial(
        lax.ppermute, axis_name=axis, perm=[(i, i ^ mask) for i in range(size)]
    )


core_flip = flip("sub", 4, 1)
ylo_flip = flip("sub", 4, 2)
yhi_flip = flip("pcol", 8, 4)


def x_step(value, step):
    pairs = [(i, i // 4 * 4 + (i % 4 + step) % 4) for i in range(8)]
    return lax.ppermute(value, "pcol", pairs)


def pcol_gather(copies):
    return lax.all_to_all(copies, "pcol", 0, 0, tiled=True)


def pcol_steps(own):
    flip_own = yhi_flip(own)
    below, above = x_step(own, 1), x_step(own, -1)
    below_flip, above_flip = x_step(flip_own, 1), x_step(flip_own, -1)
    far, far_flip = x_step(below, 1), x_step(above_flip, -1)
    return [own, flip_own, below, below_flip, far, far_flip, above, above_flip]


def z_step(value, step):
    return lax.ppermute(value, "prow", [(i, (i + step) % 8) for i in range(8)])


def call(kernel, outs, ins, scratch=(), flops=0, smem=0, parts=0, moved=None, limit=60):
    whole = len(ins) - smem - parts
    if moved is None:
        moved = sum(o.size * o.dtype.itemsize for o in list(outs) + list(ins))
    return pl.pallas_call(
        kernel,
        out_shape=tuple(outs),
        in_specs=[SMEM] * smem + [VMEM] * whole + [ANY] * parts,
        out_specs=tuple([VMEM] * len(outs)),
        scratch_shapes=list(scratch),
        compiler_params=pltpu.CompilerParams(vmem_limit_bytes=limit * 1024 * 1024),
        cost_estimate=pl.CostEstimate(flops=flops, bytes_accessed=moved, transcendentals=0),
    )(*ins)


def sds(*shape, dtype=F32):
    return jax.ShapeDtypeStruct(shape, dtype)


def split(value):
    high = value.astype(BF16)
    return high, (value - high.astype(F32)).astype(BF16)


def mm(a, b):
    return jnp.dot(a, b, preferred_element_type=F32)


def mm3(ah, al, bh, bl):
    return mm(ah, bh) + (mm(ah, bl) + mm(al, bh))


def select(hot, value):
    first = value.astype(BF16)
    rest = value - first.astype(F32)
    second = rest.astype(BF16)
    third = (rest - second.astype(F32)).astype(BF16)
    return mm(hot, first) + (mm(hot, second) + mm(hot, third))


def hot_rows(order, meta, held):
    sub, pcol = meta[0], meta[1]
    x, yhi = pcol & 3, pcol >> 2
    if held == "parent":
        owner = order >> 4
        pos = (((owner >> 3) ^ sub) & 1) * 2 + (((owner >> 4) ^ (sub >> 1)) & 1)
        pos = pos * 8 + ((x - owner) & 3) * 2 + (((owner >> 2) ^ yhi) & 1)
        pos = pos * PP + (order & (PP - 1))
    elif held == "left":
        owner = order >> 6
        pos = ((x - owner) & 3) * 2 * N + (((owner >> 2) ^ yhi) & 1) * N + (order & (N - 1))
    else:
        pos = order
    down = jnp.broadcast_to(pos.astype(F32), (BLK, PB)).T
    lanes = lax.broadcasted_iota(jnp.int32, (PB, BLK), 1)
    parts = []
    for c in range(PB // BLK):
        hit = down == (lanes + c * BLK).astype(F32)
        parts.append(jnp.where(hit, 1.0, 0.0).astype(BF16))
    return jnp.concatenate(parts, 1)


def series(panel_t, hot, ph, pw, th, tl, tf):
    eye = (
        lax.broadcasted_iota(jnp.int32, (PB, PB), 0) == lax.broadcasted_iota(jnp.int32, (PB, PB), 1)
    )
    picked = select(hot, panel_t)
    diag = jnp.sum(jnp.where(eye, picked, 0.0), axis=1, keepdims=True)
    inv_diag = 1.0 / diag
    error = jnp.where(eye, 1.0, 0.0) - picked * inv_diag
    ph[...], pw[...] = split(error)
    total = jnp.where(eye, 1.0, 0.0) + error
    tf[...] = total
    th[...], tl[...] = split(total)

    @pl.loop(0, 4)
    def _(_):
        h, w = split(mm3(ph[...], pw[...], ph[...], pw[...]))
        ph[...] = h
        pw[...] = w
        new = tf[...] + mm3(ph[...], pw[...], th[...], tl[...])
        tf[...] = new
        th[...], tl[...] = split(new)

    return inv_diag


SERIES_SCRATCH = [pltpu.VMEM((PB, PB), BF16)] * 4 + [pltpu.VMEM((PB, PB), F32)]
DMAS = lambda n: pltpu.SemaphoreType.DMA((n,))
SERIES_FLOPS = 2 * PB**3 * 27


def prep_kernel(front_rows, front_cols, parent_cols, parent_rows, piece, uppers, left_t):
    corner = front_rows[:, :N].T
    for z in range(8):
        piece[z, :32, :N] = corner[:32]
        piece[z, :32, N:] = corner[32:]
        piece[z, 32:, :N] = parent_cols[: PP // 2, :N]
        piece[z, 32:, N:] = parent_cols[PP // 2 : PP, :N]
    uppers[:, :CT] = front_rows[:, N:]
    uppers[:, CT:] = parent_cols[PP:, :N].T
    left_t[:, :CT] = front_cols[N:, :N].T
    for c in range(4):
        left_t[c * PP : (c + 1) * PP, CT:] = parent_rows[:, N + c * 256 : N + (c + 1) * 256]


def prep(front, parent_t):
    first = lambda i: (0, 0)
    return pl.pallas_call(
        prep_kernel,
        out_shape=(sds(8, 40, BLK), sds(N, PT), sds(N, CT + 256)),
        grid=(1,),
        in_specs=[
            pl.BlockSpec((N, CT + N), first),
            pl.BlockSpec((CT + N, BLK), first),
            pl.BlockSpec((PP + 256, BLK), first),
            pl.BlockSpec((PP, N + PT), first),
        ],
        out_specs=(
            pl.BlockSpec((8, 40, BLK), lambda i: (0, 0, 0)),
            pl.BlockSpec((N, PT), first),
            pl.BlockSpec((N, CT + 256), first),
        ),
        compiler_params=pltpu.CompilerParams(vmem_limit_bytes=60 * 1024 * 1024),
    )(front, front, parent_t, parent_t)


def mid_kernel(pieces, *refs):
    panel = refs[-1]
    for z in range(8):
        at = slice(z * N, (z + 1) * N)
        for i in range(8):
            panel[i, :32, at] = pieces[z, :32, :N]
            panel[i, 32:N, at] = pieces[z, :32, N:]
            panel[i, N : N + PP // 2, at] = pieces[z, 32:, :N]
            panel[i, N + PP // 2 :, at] = pieces[z, 32:, N:]


def x_fetch(dest, parts, sems):
    copies, start = [], 0
    for i, part in enumerate(parts):
        rows = pl.ds(start, part.shape[0])
        source = part.at[:, pl.ds(0, dest.shape[1])]
        copies.append(pltpu.make_async_copy(source, dest.at[rows, :], sems.at[i]))
        start += part.shape[0]
    return copies


def z_fetch(dest, cols, meta, parts, offset, sems):
    copies = []
    for i, part in enumerate(parts):
        owner = (meta[2] + (8 - i if i <= 4 else i - 4)) & 7
        rows = pl.ds(pl.multiple_of(owner * N, N), N)
        source = part.at[:, pl.ds(offset, cols)]
        copies.append(pltpu.make_async_copy(source, dest.at[rows, :], sems.at[i]))
    return copies


def begin(copies):
    for copy in copies:
        copy.start()


def finish(copies):
    for copy in copies:
        copy.wait()


def child_inverse_kernel(meta, order, blocks, *refs):
    sh, sl, inv, ph, pw, tf, panel, sems = refs[3:]
    copies = x_fetch(panel, [blocks.at[i, pl.ds(0, N), :] for i in range(8)], sems)
    begin(copies)
    hot = hot_rows(order[...], meta, "panel")
    finish(copies)
    inv[...] = series(panel[...], hot, ph, pw, sh, sl, tf)


def sources(targets, want):
    source, live = jnp.int32(0), jnp.int32(0)
    for j in range(6):
        hit = jnp.where(targets[j] == want, 1, 0).astype(jnp.int32)
        source += hit * j
        live += hit
    return source, live


def row_place(row_map, p):
    return sources([row_map[0, j] & 7 for j in range(6)], p)


def col_place(meta, col_map, q):
    values = [col_map[0, j] for j in range(6)]
    return sources([((v >> 4) ^ meta[0]) * 2 + (v & 1) for v in values], q)


def schur_kernel(meta, row_map, col_map, order, inv, *refs):
    left_parts, upper_parts, (sh_in, sl_in, front_in) = refs[:8], refs[8:16], refs[16:19]
    own_lower, outs = refs[20], refs[21:25]
    left, lower_t, upper, sh, sl, front, fetched = refs[25:]
    first = x_fetch(left, left_parts, fetched.at[pl.ds(0, 8)])
    second = [
        pltpu.make_async_copy(sh_in, sh, fetched.at[16]),
        pltpu.make_async_copy(sl_in, sl, fetched.at[17]),
    ]
    third = z_fetch(upper, CT, meta, upper_parts, 0, fetched.at[pl.ds(8, 8)])
    third.append(pltpu.make_async_copy(front_in.at[pl.ds(N, CT), :], front, fetched.at[18]))
    begin(first + second + third)
    hot = hot_rows(order[...], meta, "left")
    finish(first)
    high, low = split(select(hot, left[...]) * inv[...])
    finish(second)
    lower_t[...] = mm3(sh[...], sl[...], high, low)
    own_lower[...] = lower_t[pl.ds(pl.multiple_of(meta[1] * N, N), N), :]
    finish(third)
    uh, ul = split(upper[...])
    for i in range(3):
        lh, ll = split(lower_t[:, i * 256 : (i + 1) * 256].T)
        rows = slice(i * 256, (i + 1) * 256)
        front[rows, :CT] = front[rows, N:] - mm3(lh, ll, uh, ul)
    for slot, out in enumerate(outs):
        for b in range(2):
            csrc, clive = col_place(meta, col_map, slot * 2 + b)
            for p in range(8):
                rsrc, rlive = row_place(row_map, p)
                block = front[
                    pl.ds(pl.multiple_of(rsrc * BLK, BLK), BLK),
                    pl.ds(pl.multiple_of(csrc * BLK, BLK), BLK),
                ]
                here = (slice(p * BLK, (p + 1) * BLK), slice(b * BLK, (b + 1) * BLK))
                out[here] = jnp.where(rlive * clive > 0, block, 0.0)


def parent_rows_kernel(meta, blocks, *refs):
    parts, (out, panel, left, sems) = refs[:8], refs[8:]
    copies = [
        pltpu.make_async_copy(blocks.at[:, pl.ds(N, PP), :], panel, sems.at[8])
    ]
    for i, part in enumerate(parts):
        source = part.at[:, pl.ds(CT, 256)]
        copies.append(pltpu.make_async_copy(source, left.at[i], sems.at[i]))
    begin(copies)
    finish(copies)
    x, yhi = meta[1] & 3, meta[1] >> 2
    for i in range(8):
        owner = ((yhi ^ (i & 1)) * 4) + ((x - i // 2) & 3)
        rows = slice(i * PP, (i + 1) * PP)
        out[rows, :PB] = panel[owner]
        for c in range(4):
            at = slice(PB + c * 256, PB + (c + 1) * 256)
            out[rows, at] = left[i, c * PP : (c + 1) * PP, :]


def parent_kernel(meta, order, *refs):
    upper_parts, halves, tops, parent_t = refs[:8], refs[8:12], refs[12:14], refs[14]
    lower_out, out, ph, pw, th, tl, tf, whole, upper, near, zero, front, sems = refs[15:]
    first = x_fetch(whole, halves, sems.at[pl.ds(0, 4)])
    second = z_fetch(upper, 256, meta, upper_parts, CT, sems.at[pl.ds(4, 8)])
    second.append(pltpu.make_async_copy(tops[0], near, sems.at[12]))
    second.append(pltpu.make_async_copy(tops[1], zero, sems.at[13]))
    second.append(pltpu.make_async_copy(parent_t.at[pl.ds(PP, 256), :], front, sems.at[14]))
    begin(first + second)
    hot = hot_rows(order[...], meta, "parent")
    finish(first)
    inv = series(whole[:, :PB], hot, ph, pw, th, tl, tf)
    high, low = split(select(hot, whole[:, PB:]) * inv)
    whole[:, PB:] = mm3(th[...], tl[...], high, low)
    at = pl.multiple_of((meta[0] * 8 + meta[1]) * PP, PP)
    lower_out[...] = whole[pl.ds(at, PP), PB:]
    finish(second)
    uh, ul = split(upper[...])
    for p in range(4):
        h, w = split(whole[:, PB + p * 256 : PB + (p + 1) * 256].T)
        rows = slice(p * 256, (p + 1) * 256)
        base = front[:, N + p * 256 : N + (p + 1) * 256].T
        out[rows, :] = (base + zero[rows, :] + near[rows, :]) - mm3(h, w, uh, ul)


def body(child_front, child_order, parent_front, parent_order, row_map, col_map):
    sub = lax.axis_index("sub")
    prow = lax.axis_index("prow")
    pcol = lax.axis_index("pcol")
    front = child_front[0]
    parent_t = parent_front.T
    meta = jnp.stack([sub, pcol, prow]).astype(jnp.int32)

    piece, uppers, left_t = prep(front, parent_t)
    lows = [z_step(uppers, 1)]
    highs = [z_step(uppers, -1)]
    for _ in range(2):
        lows.append(z_step(lows[-1], 1))
        highs.append(z_step(highs[-1], -1))
    lows.append(z_step(lows[-1], 1))
    upper_parts = [uppers] + lows + highs

    pieces = lax.all_to_all(piece, "prow", 0, 0, tiled=True)
    left_parts = pcol_steps(left_t)
    ties = [left_parts[i] for i in (1, 2, 3, 4, 6, 7)] + [lows[0], highs[0]]
    (panel,) = call(
        mid_kernel, [sds(8, N + PP, PB)], [pieces] + ties, parts=len(ties)
    )
    panel = pcol_gather(panel)
    (parent_one,) = call(
        parent_rows_kernel,
        [sds(8 * PP, PB + PT)],
        [meta, panel] + left_parts,
        [pltpu.VMEM((8, PP, PB), F32), pltpu.VMEM((8, N, 256), F32), DMAS(9)],
        smem=1,
        parts=9,
    )
    parent_two = ylo_flip(parent_one)

    sh, sl, inv = call(
        child_inverse_kernel,
        [sds(PB, PB, dtype=BF16), sds(PB, PB, dtype=BF16), sds(PB, 1)],
        [meta, child_order, panel, parent_one, lows[2], highs[2]],
        [pltpu.VMEM((PB, PB), BF16)] * 2 + [pltpu.VMEM((PB, PB), F32)] * 2
        + [DMAS(8)],
        flops=SERIES_FLOPS,
        smem=1,
        parts=4,
    )
    own_lower, *terms = call(
        schur_kernel,
        [sds(N, CT)] + [sds(PT, 256)] * 4,
        [meta, row_map, col_map, child_order, inv]
        + left_parts
        + upper_parts
        + [sh, sl, front, parent_two],
        [pltpu.VMEM((PB, CT), F32)] * 3
        + [pltpu.VMEM((PB, PB), BF16)] * 2
        + [pltpu.VMEM((CT, CT + N), F32), DMAS(19)],
        flops=2 * PB * PB * CT * 6 + 2 * CT * PB * CT * 3,
        smem=3,
        parts=20,
    )
    over = core_flip(terms[3])
    near = core_flip(terms[1])
    far = ylo_flip(terms[2] + over)

    halves = [parent_one, parent_two, core_flip(parent_one), core_flip(parent_two)]
    parent_lower, partial = call(
        parent_kernel,
        [sds(PP, PT), sds(PT, 256)],
        [meta, parent_order[None]]
        + upper_parts
        + halves
        + [near, terms[0], parent_t],
        SERIES_SCRATCH
        + [pltpu.VMEM((PB, PB + PT), F32), pltpu.VMEM((PB, 256), F32)]
        + [pltpu.VMEM((PT, 256), F32)] * 2
        + [pltpu.VMEM((256, N + PT), F32), DMAS(15)],
        parts=15,
        moved=1024,
        flops=PB,
        smem=1,
    )
    return (own_lower.T[None], parent_lower.T, partial + far)


def solution(mesh):
    placed = (
        P("sub", "prow", "pcol"),
        P("sub", None),
        P("prow", ("sub", "pcol")),
        P(),
        P("sub", "prow"),
        P("sub", "pcol"),
    )
    return jax.shard_map(
        body,
        mesh=mesh,
        in_specs=placed,
        out_specs=(
            P("sub", "prow", "pcol"),
            P("prow", ("sub", "pcol")),
            P("prow", ("sub", "pcol")),
        ),
        check_vma=False,
    )
```

time: 1080 us -> 129 us (0.12)
  waiting for transfers between devices: 920 us -> 31.9 us
  matrix products: 68 us -> 0 us
  Pallas kernels: 0 us -> 48.9 us
  local copies, waits for them, and re-layouts: 52 us -> 5.43 us
  starting transfers between devices: 0.25 us -> 37.2 us
  blocking collectives: 21.3 us -> 0 us
  between operations: 14.7 us -> 0.88 us
    all_gather x5 -> x0, waiting for transfers between devices: 880 us -> none  [the longest x1 656 us: body(): lax.all_gather(parent_front[:child_rows, :parent_piv][None], ('sub', 'pro...]
    dot_general x26 -> x0, matrix products: 68 us -> none  [the longest x10 20.3 us: inverse_of(): jnp.dot(panel_block, estimate, precision=HIGH, preferred_element_type=jnp...]
    pallas_call x0 -> x6, Pallas kernels: none -> 48.9 us  [the longest x5 46.6 us: call(): pl.pallas_call(kernel, out_shape=tuple(outs), in_specs=[SMEM] * smem + [V...]
    reduce_scatter x1 -> x0, waiting for transfers between devices: 39.9 us -> none  [body(): lax.psum_scatter(placed, 'sub', scatter_dimension=1, tiled=True)]
    ppermute x0 -> x20, waiting for transfers between devices: none -> 30.3 us  [the longest x6 12.7 us: x_step(): return lax.ppermute(value, 'pcol', pairs)]
    ppermute x0 -> x20, starting transfers between devices: none -> 25.3 us  [the longest x7 8.11 us: z_step(): return lax.ppermute(value, 'prow', [(i, (i + step) % 8) for i in range(8)])]
    gather x6 -> x0, local copies, waits for them, and re-layouts: 22.2 us -> none  [the longest x2 9.6 us: inverse_of(): estimate = jnp.diag(1.0 / jnp.diagonal(panel_block))]
    all_gather x1 -> x0, blocking collectives: 21.3 us -> none  [body(): lax.all_gather(parent_front[:child_rows, parent_piv:], 'prow', axis=0, ti...]
  transfers between devices with their start and end apart: 6 -> 22, of which waited for: 6 -> 10; matrix products, arithmetic and copies ran while one was open for 10% -> 2% of each run, Pallas kernels for 0% -> 25%
where the time goes in v1:
time: 129 us
  Pallas kernels  48.9 us (38%)
  starting transfers between devices  37.2 us (29%)
  waiting for transfers between devices  31.9 us (25%)
  local copies, waits for them, and re-layouts  5.43 us (4%)
  other arithmetic  4.41 us (3%)
    pallas_call x5, Pallas kernels, call(): pl.pallas_call(kernel, out_shape=tuple(outs), in_specs=[SMEM] * smem + [V...  46.6 us
    ppermute x6, waiting for transfers between devices, x_step(): return lax.ppermute(value, 'pcol', pairs)  12.7 us
    ppermute x7, waiting for transfers between devices, z_step(): return lax.ppermute(value, 'prow', [(i, (i + step) % 8) for i in range(8)])  8.78 us
    all_to_all x1, starting transfers between devices, body(): pieces = lax.all_to_all(piece, 'prow', 0, 0, tiled=True)  8.19 us
    ppermute x7, starting transfers between devices, z_step(): return lax.ppermute(value, 'prow', [(i, (i + step) % 8) for i in range(8)])  8.11 us
    ppermute x6, starting transfers between devices, x_step(): return lax.ppermute(value, 'pcol', pairs)  6.74 us
    unnamed x50, local copies, waits for them, and re-layouts  5.43 us
    ppermute x1, starting transfers between devices, body(): over = core_flip(terms[3])  4.64 us
  transfers between devices with their start and end apart: 22, of which 10 were waited for; matrix products, arithmetic and copies ran while one was open for 2% of the time, Pallas kernels for 25%

profile of v1, /device:TPU:1, one launch (start us, length us, event | category | flops | bytes accessed | tf_op | source)
XLA Modules:
  0.0 128.7 jit_solution(2776642335483359369)
XLA Ops:
  0.6 2.3 %shard_map.85 = (f32[8,40,128]{2,1,0:T(8,128)}, f32[64,1024]{1,0:T(8,128)}, f32[64,1024]{1,0:T(8,128)}) custom-call(f32[832,832]{1,0:T(8,128)} %bitcast.10, f32[832,832]{1,0:T(8,128)} %bitcast.11, f32[272,1088]{1,0:T(8,128)} %bitcast.13, f32[272,1088]{1,0:T(8,128)} %bitcast.14), custom_call_target="tpu_custom_call" | custom-call | tf_op jit(solution)/shard_map/pallas_call | solution.py:163
  2.9 3.7 %collective-permute-start = (f32[64,1024]{1,0:T(8,128)}, f32[64,1024]{1,0:T(8,128)S(1)}, u32[]{:S(2)}, u32[]{:S(2)}) collective-permute-start(f32[64,1024]{1,0:T(8,128)} %get-tuple-element.17.refs_0_), channel_id=1, source_target_pairs={{0,4},{1,5},{2,6},{3,7},{4,0},{5,1},{6,2},{7,3},{8,12},{9,13},{10,... | collective-permute-start | bytes 786440 | tf_op jit(solution)/shard_map/ppermute | solution.py:44
  6.7 1.2 collective-permute-start.1
  7.9 1.5 %collective-permute-start.4 = (f32[64,1024]{1,0:T(8,128)}, f32[64,1024]{1,0:T(8,128)S(1)}, u32[]{:S(2)}, u32[]{:S(2)}) collective-permute-start(f32[64,1024]{1,0:T(8,128)} %get-tuple-element.17.refs_0_), channel_id=1, source_target_pairs={{0,3},{1,0},{2,1},{3,2},{4,7},{5,4},{6,5},{7,6},{8,11},{9,8},{10,9... | collective-permute-start | bytes 786440 | tf_op jit(solution)/shard_map/ppermute | solution.py:36
  9.3 8.2 %all-to-all-start = ((f32[8,40,128]{2,1,0:T(8,128)}), f32[8,40,128]{2,1,0:T(8,128)S(1)}, u32[]{:S(2)}, u32[]{:S(2)}) async-start(f32[8,40,128]{2,1,0:T(8,128)} %get-tuple-element.16), calls=%async_computation | async-start | bytes 327680 | tf_op jit(solution)/shard_map/all_to_all | solution.py:349
  17.5 1.5 %collective-permute-start.6 = (f32[64,1024]{1,0:T(8,128)}, f32[64,1024]{1,0:T(8,128)S(1)}, u32[]{:S(2)}, u32[]{:S(2)}) collective-permute-start(f32[64,1024]{1,0:T(8,128)} %get-tuple-element.18.refs_8_.refs_0_), channel_id=1, source_target_pairs={{0,8},{8,16},{16,24},{24,32},{32,40},{40,48},{48,56},{56,0},{1,9},... | collective-permute-start | bytes 786440 | tf_op jit(solution)/shard_map/ppermute | solution.py:52
  19.0 1.2 collective-permute-start.7
  20.2 0.0 collective-permute-done.refs_0_.refs_1_
  20.2 1.3 collective-permute-start.5
  21.5 0.0 collective-permute-done.1.refs_1_.refs_2_
  21.5 0.2 collective-permute-start.2
  21.7 0.0 collective-permute-done.4.refs_4_.refs_6_
  21.7 0.1 collective-permute-start.3
  21.8 7.5 %collective-permute-done.6.refs_6_.refs_9_.refs_1_ = f32[64,1024]{1,0:T(8,128)S(1)} collective-permute-done((f32[64,1024]{1,0:T(8,128)}, f32[64,1024]{1,0:T(8,128)S(1)}, u32[]{:S(2)}, u32[]{:S(2)}) %collective-permute-start.6) | collective-permute-done | bytes 262176 | tf_op jit(solution)/shard_map/ppermute | solution.py:52
  29.3 0.0 collective-permute-done.7.refs_7_.refs_13_.refs_5_
  29.3 0.0 all-to-all-done.pieces
  29.3 0.0 copy-start.18
  29.4 0.0 collective-permute-done.5.refs_5_.refs_7_
  29.4 0.0 collective-permute-done.2.refs_2_.refs_3_
  29.4 4.1 %collective-permute-done.3.refs_3_.refs_4_ = f32[64,1024]{1,0:T(8,128)S(1)} collective-permute-done((f32[64,1024]{1,0:T(8,128)S(1)}, f32[64,1024]{1,0:T(8,128)S(1)}, u32[]{:S(2)}, u32[]{:S(2)}) %collective-permute-start.3) | collective-permute-done | bytes 262176 | tf_op jit(solution)/shard_map/ppermute | solution.py:36
  33.5 0.0 copy-done.7
  33.6 0.7 copy-done.12
  34.3 2.4 %shard_map.86 = f32[8,80,512]{2,1,0:T(8,128)} custom-call(f32[8,40,128]{2,1,0:T(8,128)} %copy-done.18, f32[64,1024]{1,0:T(8,128)} %copy-done.6, f32[64,1024]{1,0:T(8,128)} %copy-done.7, f32[64,1024]{1,0:T(8,128)} %copy-done.11, f32[64,1024]{1,0:T(8,128)} %copy-done.12, f32[64,1024]{1,0:T(8,128)} %copy-done.8, f32[64,1024]{1,0:T(8,128)} %copy-done.9, ...), custom_call_target="tpu_custom_call" | custom-call | bytes 3571712 | tf_op jit(solution)/shard_map/pallas_call | solution.py:59
  36.7 3.7 %all-to-all-start.1 = ((f32[8,80,512]{2,1,0:T(8,128)}), f32[8,80,512]{2,1,0:T(8,128)S(1)}, u32[]{:S(2)}, u32[]{:S(2)}) async-start(f32[8,80,512]{2,1,0:T(8,128)} %shard_map.86), calls=%async_computation.1 | async-start | bytes 2621440 | tf_op jit(solution)/shard_map/all_to_all | solution.py:40
  40.4 0.1 collective-permute-start.9
  40.5 2.7 %collective-permute-start.11 = (f32[64,1024]{1,0:T(8,128)S(1)}, f32[64,1024]{1,0:T(8,128)S(1)}, u32[]{:S(2)}, u32[]{:S(2)}) collective-permute-start(f32[64,1024]{1,0:T(8,128)S(1)} %copy-done.5), channel_id=1, source_target_pairs={{0,56},{8,0},{16,8},{24,16},{32,24},{40,32},{48,40},{56,48},{1,57}... | collective-permute-start | bytes 786440 | tf_op jit(solution)/shard_map/ppermute | solution.py:52
  43.2 0.0 copy-done.10
  43.2 2.5 %collective-permute-start.8 = (f32[64,1024]{1,0:T(8,128)S(1)}, f32[64,1024]{1,0:T(8,128)S(1)}, u32[]{:S(2)}, u32[]{:S(2)}) collective-permute-start(f32[64,1024]{1,0:T(8,128)S(1)} %copy-done.10), channel_id=1, source_target_pairs={{0,3},{1,0},{2,1},{3,2},{4,7},{5,4},{6,5},{7,6},{8,11},{9,8},{10,9... | collective-permute-start | bytes 786440 | tf_op jit(solution)/shard_map/ppermute | solution.py:36
  45.7 1.3 collective-permute-done.9.refs_10_.refs_2_
  46.9 0.0 collective-permute-start.10
  46.9 0.0 collective-permute-done.11.refs_14_.refs_6_
  46.9 0.0 copy-start.20
  47.0 2.7 %collective-permute-start.12 = (f32[64,1024]{1,0:T(8,128)S(1)}, f32[64,1024]{1,0:T(8,128)S(1)}, u32[]{:S(2)}, u32[]{:S(2)}) collective-permute-start(f32[64,1024]{1,0:T(8,128)S(1)} %collective-permute-done.11.refs_14_.refs_6_), channel_id=1, source_target_pairs={{0,56},{8,0},{16,8},{24,16},{32,24},{40,32},{48,40},{56,48},{1,57}... | collective-permute-start | bytes 786440 | tf_op jit(solution)/shard_map/ppermute | solution.py:52
  49.6 0.6 pad_add_fusion.meta
  50.2 8.6 %collective-permute-done.8.refs_5_ = f32[64,1024]{1,0:T(8,128)S(1)} collective-permute-done((f32[64,1024]{1,0:T(8,128)S(1)}, f32[64,1024]{1,0:T(8,128)S(1)}, u32[]{:S(2)}, u32[]{:S(2)}) %collective-permute-start.8) | collective-permute-done | bytes 262176 | tf_op jit(solution)/shard_map/ppermute | solution.py:36
  58.8 1.6 %all-to-all-done.1.blocks = f32[8,80,512]{2,1,0:T(8,128)S(1)} async-done(((f32[8,80,512]{2,1,0:T(8,128)}), f32[8,80,512]{2,1,0:T(8,128)S(1)}, u32[]{:S(2)}, u32[]{:S(2)}) %all-to-all-start.1) | async-done | bytes 1310752 | tf_op jit(solution)/shard_map/all_to_all | solution.py:40
  60.4 1.1 copy-done
  61.5 2.8 %shard_map.87.refs_0_.refs_8_ = f32[128,1536]{1,0:T(8,128)} custom-call(s32[3]{0:T(128)} %pad_add_fusion.meta, f32[8,80,512]{2,1,0:T(8,128)} %copy-done, f32[64,1024]{1,0:T(8,128)} %get-tuple-element.17.refs_0_, f32[64,1024]{1,0:T(8,128)} %copy-done.6, f32[64,1024]{1,0:T(8,128)} %copy-done.7, f32[64,1024]{1,0:T(8,128)} %copy-done.11, f32[64,1024]{1,0:T(8,128)} %copy-done.12, ...), custom_call_target="tpu_custom_call" | custom-call | bytes 4194316 | tf_op jit(solution)/shard_map/pallas_call | solution.py:59
  64.3 0.5 collective-permute-start.14
  64.8 0.0 collective-permute-done.10.refs_1_.refs_11_.refs_3_
  64.8 0.0 collective-permute-start.13
  64.8 0.0 collective-permute-done.12.refs_2_.refs_15_.refs_7_
  64.8 0.7 copy-done.21
  65.5 0.7 copy-done.22
  66.2 11.8 %shard_map.88 = (bf16[512,512]{1,0:T(8,128)(2,1)}, bf16[512,512]{1,0:T(8,128)(2,1)}, f32[512,1]{1,0:T(8,128)}) custom-call(s32[3]{0:T(128)} %pad_add_fusion.meta, s32[1,512]{1,0:T(1,128)} %order.3, f32[8,80,512]{2,1,0:T(8,128)} %copy-done, f32[128,1536]{1,0:T(8,128)} %shard_map.87.refs_0_.refs_8_, f32[64,1024]{1,0:T(8,128)} %copy-done.21, f32[64,1024]{1,0:T(8,128)} %copy-done.22), custom_call_target="tpu_custom_call" | custom-call | flops 7247757312 | bytes 3674124 | tf_op jit(solution)/shard_map/pallas_call | solution.py:59
  78.0 0.0 collective-permute-done.13.refs_12_.refs_4_
  78.1 1.9 %collective-permute-done.14.refs_19_.refs_9_ = f32[128,1536]{1,0:T(8,128)S(1)} collective-permute-done((f32[128,1536]{1,0:T(8,128)}, f32[128,1536]{1,0:T(8,128)S(1)}, u32[]{:S(2)}, u32[]{:S(2)}) %collective-permute-start.14) | collective-permute-done | bytes 786464 | tf_op jit(solution)/shard_map/ppermute | solution.py:364
  80.0 0.9 copy-done.14
  80.9 12.4 %shard_map.89 = (f32[64,768]{1,0:T(8,128)}, f32[1024,256]{1,0:T(8,128)}, f32[1024,256]{1,0:T(8,128)}, f32[1024,256]{1,0:T(8,128)}, f32[1024,256]{1,0:T(8,128)}) custom-call(s32[3]{0:T(128)} %pad_add_fusion.meta, s32[1,6]{1,0:T(1,128)} %row_map.1, s32[1,6]{1,0:T(1,128)} %col_map.1, s32[1,512]{1,0:T(1,128)} %order.3, f32[512,1]{1,0:T(8,128)} %get-tuple-element.19.inv, ...), custom_call_target="tpu_custom_call" | custom-call | flops 4227858432 | bytes 13193276 | tf_op jit(solution)/shard_map/pallas_call | solution.py:59
  93.3 4.6 %collective-permute-start.18 = (f32[1024,256]{1,0:T(8,128)}, f32[1024,256]{1,0:T(8,128)S(1)}, u32[]{:S(2)}, u32[]{:S(2)}) collective-permute-start(f32[1024,256]{1,0:T(8,128)} %get-tuple-element.28), channel_id=1, source_target_pairs={{0,64},{64,0},{128,192},{192,128},{1,65},{65,1},{129,193},{193,129... | collective-permute-start | bytes 3145736 | tf_op jit(solution)/shard_map/ppermute | solution.py:390
  97.9 0.1 collective-permute-start.17
  98.0 2.4 %collective-permute-done.18 = f32[1024,256]{1,0:T(8,128)S(1)} collective-permute-done((f32[1024,256]{1,0:T(8,128)}, f32[1024,256]{1,0:T(8,128)S(1)}, u32[]{:S(2)}, u32[]{:S(2)}) %collective-permute-start.18) | collective-permute-done | bytes 1048608 | tf_op jit(solution)/shard_map/ppermute | solution.py:390
  100.4 1.5 %add.6 = f32[1024,256]{1,0:T(8,128)S(1)} add(f32[1024,256]{1,0:T(8,128)} %get-tuple-element.27, f32[1024,256]{1,0:T(8,128)S(1)} %collective-permute-done.18) | non-fusion elementwise | flops 262144 | bytes 3145728 | tf_op jit(solution)/shard_map/add | solution.py:392
  101.9 0.5 collective-permute-start.19
  102.4 0.7 collective-permute-start.15
  103.1 0.3 collective-permute-start.16
  103.4 1.6 %collective-permute-done.15.refs_10_ = f32[128,1536]{1,0:T(8,128)S(1)} collective-permute-done((f32[128,1536]{1,0:T(8,128)S(1)}, f32[128,1536]{1,0:T(8,128)S(1)}, u32[]{:S(2)}, u32[]{:S(2)}) %collective-permute-start.15) | collective-permute-done | bytes 786464 | tf_op jit(solution)/shard_map/ppermute | solution.py:394
  105.0 1.1 collective-permute-done.16.refs_11_
  106.1 0.0 collective-permute-done.17.refs_12_
  106.1 0.9 copy-done.17
  107.0 0.3 copy-done.13
  107.3 17.2 %shard_map.90 = (f32[16,1024]{1,0:T(8,128)}, f32[1024,256]{1,0:T(8,128)}) custom-call(s32[3]{0:T(128)} %pad_add_fusion.meta, s32[1,512]{1,0:T(1,128)} %bitcast.16, f32[64,1024]{1,0:T(8,128)} %get-tuple-element.18.refs_8_.refs_0_, f32[64,1024]{1,0:T(8,128)} %copy-done.2, f32[64,1024]{1,0:T(8,128)} %copy-done.19, f32[64,1024]{1,0:T(8,128)} %copy-done.21, ...), custom_call_target="tpu_custom_call" | custom-call | flops 512 | bytes 1024 | tf_op jit(solution)/shard_map/pallas_call | solution.py:59
  124.5 1.8 %collective-permute-done.19 = f32[1024,256]{1,0:T(8,128)S(1)} collective-permute-done((f32[1024,256]{1,0:T(8,128)S(1)}, f32[1024,256]{1,0:T(8,128)S(1)}, u32[]{:S(2)}, u32[]{:S(2)}) %collective-permute-start.19) | collective-permute-done | bytes 1048608 | tf_op jit(solution)/shard_map/ppermute | solution.py:392
  126.4 2.3 %add.7 = f32[1024,256]{1,0:T(8,128)} add(f32[1024,256]{1,0:T(8,128)} %get-tuple-element.26, f32[1024,256]{1,0:T(8,128)S(1)} %collective-permute-done.19) | non-fusion elementwise | flops 262144 | bytes 3145728 | tf_op jit(solution)/shard_map/add | solution.py:411
  (39 shorter events, 0.1 us)
Async XLA Ops:
  2.9 17.3 %collective-permute-start = (f32[64,1024]{1,0:T(8,128)}, f32[64,1024]{1,0:T(8,128)S(1)}, u32[]{:S(2)}, u32[]{:S(2)}) collective-permute-start(f32[64,1024]{1,0:T(8,128)} %get-tuple-element.17.refs_0_), channel_id=1, source_target_pairs={{0,4},{1,5},{2,6},{3,7},{4,0},{5,1},{6,2},{7,3},{8,12},{9,13},{10,... | collective-permute-start | bytes 786440 | tf_op jit(solution)/shard_map/ppermute | solution.py:44
  6.7 14.8 %collective-permute-start.1 = (f32[64,1024]{1,0:T(8,128)}, f32[64,1024]{1,0:T(8,128)S(1)}, u32[]{:S(2)}, u32[]{:S(2)}) collective-permute-start(f32[64,1024]{1,0:T(8,128)} %get-tuple-element.17.refs_0_), channel_id=1, source_target_pairs={{0,1},{1,2},{2,3},{3,0},{4,5},{5,6},{6,7},{7,4},{8,9},{9,10},{10,1... | collective-permute-start | bytes 786440 | tf_op jit(solution)/shard_map/ppermute | solution.py:36
  7.9 13.8 %collective-permute-start.4 = (f32[64,1024]{1,0:T(8,128)}, f32[64,1024]{1,0:T(8,128)S(1)}, u32[]{:S(2)}, u32[]{:S(2)}) collective-permute-start(f32[64,1024]{1,0:T(8,128)} %get-tuple-element.17.refs_0_), channel_id=1, source_target_pairs={{0,3},{1,0},{2,1},{3,2},{4,7},{5,4},{6,5},{7,6},{8,11},{9,8},{10,9... | collective-permute-start | bytes 786440 | tf_op jit(solution)/shard_map/ppermute | solution.py:36
  9.3 20.0 %all-to-all-start = ((f32[8,40,128]{2,1,0:T(8,128)}), f32[8,40,128]{2,1,0:T(8,128)S(1)}, u32[]{:S(2)}, u32[]{:S(2)}) async-start(f32[8,40,128]{2,1,0:T(8,128)} %get-tuple-element.16), calls=%async_computation | async-start | bytes 327680 | tf_op jit(solution)/shard_map/all_to_all | solution.py:349
  17.5 11.8 %collective-permute-start.6 = (f32[64,1024]{1,0:T(8,128)}, f32[64,1024]{1,0:T(8,128)S(1)}, u32[]{:S(2)}, u32[]{:S(2)}) collective-permute-start(f32[64,1024]{1,0:T(8,128)} %get-tuple-element.18.refs_8_.refs_0_), channel_id=1, source_target_pairs={{0,8},{8,16},{16,24},{24,32},{32,40},{40,48},{48,56},{56,0},{1,9},... | collective-permute-start | bytes 786440 | tf_op jit(solution)/shard_map/ppermute | solution.py:52
  19.0 10.3 %collective-permute-start.7 = (f32[64,1024]{1,0:T(8,128)}, f32[64,1024]{1,0:T(8,128)S(1)}, u32[]{:S(2)}, u32[]{:S(2)}) collective-permute-start(f32[64,1024]{1,0:T(8,128)} %get-tuple-element.18.refs_8_.refs_0_), channel_id=1, source_target_pairs={{0,56},{8,0},{16,8},{24,16},{32,24},{40,32},{48,40},{56,48},{1,57}... | collective-permute-start | bytes 786440 | tf_op jit(solution)/shard_map/ppermute | solution.py:52
  20.2 13.3 %copy-start.6 = (f32[64,1024]{1,0:T(8,128)}, f32[64,1024]{1,0:T(8,128)S(1)}, u32[]{:S(2)}) copy-start(f32[64,1024]{1,0:T(8,128)S(1)} %collective-permute-done.refs_0_.refs_1_) | copy-start | bytes 786436
  20.2 9.1 %collective-permute-start.5 = (f32[64,1024]{1,0:T(8,128)S(1)}, f32[64,1024]{1,0:T(8,128)S(1)}, u32[]{:S(2)}, u32[]{:S(2)}) collective-permute-start(f32[64,1024]{1,0:T(8,128)S(1)} %collective-permute-done.refs_0_.refs_1_), channel_id=1, source_target_pairs={{0,3},{1,0},{2,1},{3,2},{4,7},{5,4},{6,5},{7,6},{8,11},{9,8},{10,9... | collective-permute-start | bytes 786440 | tf_op jit(solution)/shard_map/ppermute | solution.py:36
  21.5 12.0 %copy-start.7 = (f32[64,1024]{1,0:T(8,128)}, f32[64,1024]{1,0:T(8,128)S(1)}, u32[]{:S(2)}) copy-start(f32[64,1024]{1,0:T(8,128)S(1)} %collective-permute-done.1.refs_1_.refs_2_) | copy-start | bytes 786436
  21.5 7.9 %collective-permute-start.2 = (f32[64,1024]{1,0:T(8,128)S(1)}, f32[64,1024]{1,0:T(8,128)S(1)}, u32[]{:S(2)}, u32[]{:S(2)}) collective-permute-start(f32[64,1024]{1,0:T(8,128)S(1)} %collective-permute-done.refs_0_.refs_1_), channel_id=1, source_target_pairs={{0,1},{1,2},{2,3},{3,0},{4,5},{5,6},{6,7},{7,4},{8,9},{9,10},{10,1... | collective-permute-start | bytes 786440 | tf_op jit(solution)/shard_map/ppermute | solution.py:36
  21.7 11.8 %copy-start.8 = (f32[64,1024]{1,0:T(8,128)}, f32[64,1024]{1,0:T(8,128)S(1)}, u32[]{:S(2)}) copy-start(f32[64,1024]{1,0:T(8,128)S(1)} %collective-permute-done.4.refs_4_.refs_6_) | copy-start | bytes 786436
  21.7 11.8 %collective-permute-start.3 = (f32[64,1024]{1,0:T(8,128)S(1)}, f32[64,1024]{1,0:T(8,128)S(1)}, u32[]{:S(2)}, u32[]{:S(2)}) collective-permute-start(f32[64,1024]{1,0:T(8,128)S(1)} %collective-permute-done.1.refs_1_.refs_2_), channel_id=1, source_target_pairs={{0,1},{1,2},{2,3},{3,0},{4,5},{5,6},{6,7},{7,4},{8,9},{9,10},{10,1... | collective-permute-start | bytes 786440 | tf_op jit(solution)/shard_map/ppermute | solution.py:36
  29.3 4.2 %copy-start.2 = (f32[64,1024]{1,0:T(8,128)}, f32[64,1024]{1,0:T(8,128)S(1)}, u32[]{:S(2)}) copy-start(f32[64,1024]{1,0:T(8,128)S(1)} %collective-permute-done.6.refs_6_.refs_9_.refs_1_) | copy-start | bytes 786436
  29.3 4.2 %copy-start.4 = (f32[64,1024]{1,0:T(8,128)}, f32[64,1024]{1,0:T(8,128)S(1)}, u32[]{:S(2)}) copy-start(f32[64,1024]{1,0:T(8,128)S(1)} %collective-permute-done.7.refs_7_.refs_13_.refs_5_) | copy-start | bytes 786436
  29.3 4.2 %copy-start.18 = (f32[8,40,128]{2,1,0:T(8,128)}, f32[8,40,128]{2,1,0:T(8,128)S(1)}, u32[]{:S(2)}) copy-start(f32[8,40,128]{2,1,0:T(8,128)S(1)} %all-to-all-done.pieces) | copy-start | bytes 491524
  29.4 4.2 %copy-start.9 = (f32[64,1024]{1,0:T(8,128)}, f32[64,1024]{1,0:T(8,128)S(1)}, u32[]{:S(2)}) copy-start(f32[64,1024]{1,0:T(8,128)S(1)} %collective-permute-done.5.refs_5_.refs_7_) | copy-start | bytes 786436
  29.4 4.2 %copy-start.11 = (f32[64,1024]{1,0:T(8,128)}, f32[64,1024]{1,0:T(8,128)S(1)}, u32[]{:S(2)}) copy-start(f32[64,1024]{1,0:T(8,128)S(1)} %collective-permute-done.2.refs_2_.refs_3_) | copy-start | bytes 786436
  33.6 0.7 copy-start.12
  36.7 3.7 %copy-start.3 = (f32[64,1024]{1,0:T(8,128)S(1)}, f32[64,1024]{1,0:T(8,128)}, u32[]{:S(2)}) copy-start(f32[64,1024]{1,0:T(8,128)} %copy-done.2) | copy-start | bytes 786436
  36.7 3.8 %copy-start.5 = (f32[64,1024]{1,0:T(8,128)S(1)}, f32[64,1024]{1,0:T(8,128)}, u32[]{:S(2)}) copy-start(f32[64,1024]{1,0:T(8,128)} %copy-done.4) | copy-start | bytes 786436
  36.7 6.5 %copy-start.10 = (f32[64,1024]{1,0:T(8,128)S(1)}, f32[64,1024]{1,0:T(8,128)}, u32[]{:S(2)}) copy-start(f32[64,1024]{1,0:T(8,128)} %copy-done.9) | copy-start | bytes 786436
  36.7 23.7 %all-to-all-start.1 = ((f32[8,80,512]{2,1,0:T(8,128)}), f32[8,80,512]{2,1,0:T(8,128)S(1)}, u32[]{:S(2)}, u32[]{:S(2)}) async-start(f32[8,80,512]{2,1,0:T(8,128)} %shard_map.86), calls=%async_computation.1 | async-start | bytes 2621440 | tf_op jit(solution)/shard_map/all_to_all | solution.py:40
  40.4 6.5 %collective-permute-start.9 = (f32[64,1024]{1,0:T(8,128)S(1)}, f32[64,1024]{1,0:T(8,128)S(1)}, u32[]{:S(2)}, u32[]{:S(2)}) collective-permute-start(f32[64,1024]{1,0:T(8,128)S(1)} %copy-done.3), channel_id=1, source_target_pairs={{0,8},{8,16},{16,24},{24,32},{32,40},{40,48},{48,56},{56,0},{1,9},... | collective-permute-start | bytes 786440 | tf_op jit(solution)/shard_map/ppermute | solution.py:52
  40.5 6.4 %collective-permute-start.11 = (f32[64,1024]{1,0:T(8,128)S(1)}, f32[64,1024]{1,0:T(8,128)S(1)}, u32[]{:S(2)}, u32[]{:S(2)}) collective-permute-start(f32[64,1024]{1,0:T(8,128)S(1)} %copy-done.5), channel_id=1, source_target_pairs={{0,56},{8,0},{16,8},{24,16},{32,24},{40,32},{48,40},{56,48},{1,57}... | collective-permute-start | bytes 786440 | tf_op jit(solution)/shard_map/ppermute | solution.py:52
  43.2 15.6 %collective-permute-start.8 = (f32[64,1024]{1,0:T(8,128)S(1)}, f32[64,1024]{1,0:T(8,128)S(1)}, u32[]{:S(2)}, u32[]{:S(2)}) collective-permute-start(f32[64,1024]{1,0:T(8,128)S(1)} %copy-done.10), channel_id=1, source_target_pairs={{0,3},{1,0},{2,1},{3,2},{4,7},{5,4},{6,5},{7,6},{8,11},{9,8},{10,9... | collective-permute-start | bytes 786440 | tf_op jit(solution)/shard_map/ppermute | solution.py:36
  46.9 31.1 %copy-start.19 = (f32[64,1024]{1,0:T(8,128)}, f32[64,1024]{1,0:T(8,128)S(1)}, u32[]{:S(2)}) copy-start(f32[64,1024]{1,0:T(8,128)S(1)} %collective-permute-done.9.refs_10_.refs_2_) | copy-start | bytes 786436
  46.9 17.8 %collective-permute-start.10 = (f32[64,1024]{1,0:T(8,128)S(1)}, f32[64,1024]{1,0:T(8,128)S(1)}, u32[]{:S(2)}, u32[]{:S(2)}) collective-permute-start(f32[64,1024]{1,0:T(8,128)S(1)} %collective-permute-done.9.refs_10_.refs_2_), channel_id=1, source_target_pairs={{0,8},{8,16},{16,24},{24,32},{32,40},{40,48},{48,56},{56,0},{1,9},... | collective-permute-start | bytes 786440 | tf_op jit(solution)/shard_map/ppermute | solution.py:52
  46.9 31.1 %copy-start.20 = (f32[64,1024]{1,0:T(8,128)}, f32[64,1024]{1,0:T(8,128)S(1)}, u32[]{:S(2)}) copy-start(f32[64,1024]{1,0:T(8,128)S(1)} %collective-permute-done.11.refs_14_.refs_6_) | copy-start | bytes 786436
  47.0 17.8 %collective-permute-start.12 = (f32[64,1024]{1,0:T(8,128)S(1)}, f32[64,1024]{1,0:T(8,128)S(1)}, u32[]{:S(2)}, u32[]{:S(2)}) collective-permute-start(f32[64,1024]{1,0:T(8,128)S(1)} %collective-permute-done.11.refs_14_.refs_6_), channel_id=1, source_target_pairs={{0,56},{8,0},{16,8},{24,16},{32,24},{40,32},{48,40},{56,48},{1,57}... | collective-permute-start | bytes 786440 | tf_op jit(solution)/shard_map/ppermute | solution.py:52
  58.8 1.6 %copy-start.23 = (f32[64,1024]{1,0:T(8,128)}, f32[64,1024]{1,0:T(8,128)S(1)}, u32[]{:S(2)}) copy-start(f32[64,1024]{1,0:T(8,128)S(1)} %collective-permute-done.8.refs_5_) | copy-start | bytes 786436
  60.4 1.1 copy-start
  64.3 15.7 %collective-permute-start.14 = (f32[128,1536]{1,0:T(8,128)}, f32[128,1536]{1,0:T(8,128)S(1)}, u32[]{:S(2)}, u32[]{:S(2)}) collective-permute-start(f32[128,1536]{1,0:T(8,128)} %shard_map.87.refs_0_.refs_8_), channel_id=1, source_target_pairs={{0,128},{64,192},{128,0},{192,64},{1,129},{65,193},{129,1},{193,65... | collective-permute-start | bytes 2359304 | tf_op jit(solution)/shard_map/ppermute | solution.py:364
  64.8 0.7 copy-start.21
  64.8 13.3 %collective-permute-start.13 = (f32[64,1024]{1,0:T(8,128)S(1)}, f32[64,1024]{1,0:T(8,128)S(1)}, u32[]{:S(2)}, u32[]{:S(2)}) collective-permute-start(f32[64,1024]{1,0:T(8,128)S(1)} %collective-permute-done.10.refs_1_.refs_11_.refs_3_), channel_id=1, source_target_pairs={{0,8},{8,16},{16,24},{24,32},{32,40},{40,48},{48,56},{56,0},{1,9},... | collective-permute-start | bytes 786440 | tf_op jit(solution)/shard_map/ppermute | solution.py:52
  65.5 0.7 copy-start.22
  78.1 1.9 %copy-start.24 = (f32[64,1024]{1,0:T(8,128)}, f32[64,1024]{1,0:T(8,128)S(1)}, u32[]{:S(2)}) copy-start(f32[64,1024]{1,0:T(8,128)S(1)} %collective-permute-done.13.refs_12_.refs_4_) | copy-start | bytes 786436
  80.0 0.9 copy-start.14
  93.3 7.1 %collective-permute-start.18 = (f32[1024,256]{1,0:T(8,128)}, f32[1024,256]{1,0:T(8,128)S(1)}, u32[]{:S(2)}, u32[]{:S(2)}) collective-permute-start(f32[1024,256]{1,0:T(8,128)} %get-tuple-element.28), channel_id=1, source_target_pairs={{0,64},{64,0},{128,192},{192,128},{1,65},{65,1},{129,193},{193,129... | collective-permute-start | bytes 3145736 | tf_op jit(solution)/shard_map/ppermute | solution.py:390
  97.9 8.2 %collective-permute-start.17 = (f32[1024,256]{1,0:T(8,128)}, f32[1024,256]{1,0:T(8,128)S(1)}, u32[]{:S(2)}, u32[]{:S(2)}) collective-permute-start(f32[1024,256]{1,0:T(8,128)} %get-tuple-element.23), channel_id=1, source_target_pairs={{0,64},{64,0},{128,192},{192,128},{1,65},{65,1},{129,193},{193,129... | collective-permute-start | bytes 3145736 | tf_op jit(solution)/shard_map/ppermute | solution.py:391
  100.4 2.0 %copy-start.1 = (f32[128,1536]{1,0:T(8,128)S(1)}, f32[128,1536]{1,0:T(8,128)}, u32[]{:S(2)}) copy-start(f32[128,1536]{1,0:T(8,128)} %shard_map.87.refs_0_.refs_8_) | copy-start | bytes 2359300
  100.4 2.6 %copy-start.15 = (f32[128,1536]{1,0:T(8,128)S(1)}, f32[128,1536]{1,0:T(8,128)}, u32[]{:S(2)}) copy-start(f32[128,1536]{1,0:T(8,128)} %copy-done.14) | copy-start | bytes 2359300
  101.9 24.5 %collective-permute-start.19 = (f32[1024,256]{1,0:T(8,128)S(1)}, f32[1024,256]{1,0:T(8,128)S(1)}, u32[]{:S(2)}, u32[]{:S(2)}) collective-permute-start(f32[1024,256]{1,0:T(8,128)S(1)} %add.6), channel_id=1, source_target_pairs={{0,128},{64,192},{128,0},{192,64},{1,129},{65,193},{129,1},{193,65... | collective-permute-start | bytes 3145736 | tf_op jit(solution)/shard_map/ppermute | solution.py:392
  102.4 2.6 %collective-permute-start.15 = (f32[128,1536]{1,0:T(8,128)S(1)}, f32[128,1536]{1,0:T(8,128)S(1)}, u32[]{:S(2)}, u32[]{:S(2)}) collective-permute-start(f32[128,1536]{1,0:T(8,128)S(1)} %copy-done.1), channel_id=1, source_target_pairs={{0,64},{64,0},{128,192},{192,128},{1,65},{65,1},{129,193},{193,129... | collective-permute-start | bytes 2359304 | tf_op jit(solution)/shard_map/ppermute | solution.py:394
  103.1 3.0 %collective-permute-start.16 = (f32[128,1536]{1,0:T(8,128)S(1)}, f32[128,1536]{1,0:T(8,128)S(1)}, u32[]{:S(2)}, u32[]{:S(2)}) collective-permute-start(f32[128,1536]{1,0:T(8,128)S(1)} %copy-done.15), channel_id=1, source_target_pairs={{0,64},{64,0},{128,192},{192,128},{1,65},{65,1},{129,193},{193,129... | collective-permute-start | bytes 2359304 | tf_op jit(solution)/shard_map/ppermute | solution.py:394
  105.0 1.1 copy-start.16
  106.1 0.9 copy-start.17
  106.1 1.2 copy-start.13

commit v2 on v1

--- a/solution.py
+++ b/solution.py
@@ -17,6 +17,7 @@
 BF16 = jnp.bfloat16
 VMEM = pl.BlockSpec(memory_space=pltpu.VMEM)
 ANY = pl.BlockSpec(memory_space=pl.ANY)
+HBM = pl.BlockSpec(memory_space=pltpu.HBM)
 SMEM = pl.BlockSpec(memory_space=pltpu.SMEM)
 
 
@@ -52,14 +53,14 @@
     return lax.ppermute(value, "prow", [(i, (i + step) % 8) for i in range(8)])
 
 
-def call(kernel, outs, ins, scratch=(), flops=0, smem=0, parts=0, moved=None, limit=60):
+def call(kernel, outs, ins, scratch=(), flops=0, smem=0, parts=0, moved=None, limit=60, where=ANY):
     whole = len(ins) - smem - parts
     if moved is None:
         moved = sum(o.size * o.dtype.itemsize for o in list(outs) + list(ins))
     return pl.pallas_call(
         kernel,
         out_shape=tuple(outs),
-        in_specs=[SMEM] * smem + [VMEM] * whole + [ANY] * parts,
+        in_specs=[SMEM] * smem + [VMEM] * whole + [where] * parts,
         out_specs=tuple([VMEM] * len(outs)),
         scratch_shapes=list(scratch),
         compiler_params=pltpu.CompilerParams(vmem_limit_bytes=limit * 1024 * 1024),
@@ -81,7 +82,7 @@
 
 
 def mm3(ah, al, bh, bl):
-    return mm(ah, bh) + (mm(ah, bl) + mm(al, bh))
+    return mm(jnp.concatenate([ah, ah, al], 1), jnp.concatenate([bh, bl, bh], 0))
 
 
 def select(hot, value):
@@ -348,7 +349,7 @@
 
     pieces = lax.all_to_all(piece, "prow", 0, 0, tiled=True)
     left_parts = pcol_steps(left_t)
-    ties = [left_parts[i] for i in (1, 2, 3, 4, 6, 7)] + [lows[0], highs[0]]
+    ties = [left_parts[i] for i in (1, 2, 3, 4, 6, 7)]
     (panel,) = call(
         mid_kernel, [sds(8, N + PP, PB)], [pieces] + ties, parts=len(ties)
     )
@@ -405,6 +406,8 @@
         + [pltpu.VMEM((256, N + PT), F32), DMAS(15)],
         parts=15,
         moved=1024,
+        limit=40,
+        where=HBM,
         flops=PB,
         smem=1,
     )

time: 129 us -> 125 us (0.969)
  Pallas kernels: 48.9 us -> 45.4 us
    pallas_call x5, Pallas kernels: 46.6 us -> 43.1 us  [call(): pl.pallas_call(kernel, out_shape=tuple(outs), in_specs=[SMEM] * smem + [V...]
    ppermute x7, waiting for transfers between devices: 8.78 us -> 5.51 us  [z_step(): return lax.ppermute(value, 'prow', [(i, (i + step) % 8) for i in range(8)])]
    all_to_all x1, waiting for transfers between devices: 0.01 us -> 1.87 us  [body(): pieces = lax.all_to_all(piece, 'prow', 0, 0, tiled=True)]
    ppermute x1, waiting for transfers between devices: 1.6 us -> 2.99 us  [body(): core_flip(parent_one)]
    unnamed x50 -> x62, local copies, waits for them, and re-layouts: 5.43 us -> 5.6 us
  transfers between devices with their start and end apart: 22 -> 22, of which waited for: 10 -> 15; matrix products, arithmetic and copies ran while one was open for 2% -> 2% of each run, Pallas kernels for 25% -> 24%
where the time goes in v2:
time: 125 us; the launch traced here: 124 us
  Pallas kernels  45.4 us (36%)
  starting transfers between devices  37.9 us (30%)
  waiting for transfers between devices  31.1 us (25%)
  local copies, waits for them, and re-layouts  5.6 us (4%)
  other arithmetic  3.23 us (3%)
    pallas_call x5, Pallas kernels, call(): pl.pallas_call(kernel, out_shape=tuple(outs), in_specs=[SMEM] * smem + [V...  43.1 us
    ppermute x6, waiting for transfers between devices, x_step(): return lax.ppermute(value, 'pcol', pairs)  12.6 us
    ppermute x7, starting transfers between devices, z_step(): return lax.ppermute(value, 'prow', [(i, (i + step) % 8) for i in range(8)])  9.17 us
    all_to_all x1, starting transfers between devices, body(): pieces = lax.all_to_all(piece, 'prow', 0, 0, tiled=True)  8.19 us
    ppermute x6, starting transfers between devices, x_step(): return lax.ppermute(value, 'pcol', pairs)  6.81 us
    unnamed x62, local copies, waits for them, and re-layouts  5.6 us
    ppermute x7, waiting for transfers between devices, z_step(): return lax.ppermute(value, 'prow', [(i, (i + step) % 8) for i in range(8)])  5.51 us
    ppermute x1, starting transfers between devices, body(): over = core_flip(terms[3])  4.52 us
  transfers between devices with their start and end apart: 22, of which 15 were waited for; matrix products, arithmetic and copies ran while one was open for 2% of the time, Pallas kernels for 24%

profile of v2, /device:TPU:1, one launch (start us, length us, event | category | flops | bytes accessed | tf_op | source)
XLA Modules:
  0.0 124.1 jit_solution(3019904591736917337)
XLA Ops:
  0.6 2.3 %shard_map.85 = (f32[8,40,128]{2,1,0:T(8,128)}, f32[64,1024]{1,0:T(8,128)}, f32[64,1024]{1,0:T(8,128)}) custom-call(f32[832,832]{1,0:T(8,128)} %bitcast.14, f32[832,832]{1,0:T(8,128)} %bitcast.15, f32[272,1088]{1,0:T(8,128)} %bitcast.10, f32[272,1088]{1,0:T(8,128)} %bitcast.11), custom_call_target="tpu_custom_call" | custom-call | tf_op jit(solution)/shard_map/pallas_call | solution.py:164
  3.0 3.7 %collective-permute-start = (f32[64,1024]{1,0:T(8,128)}, f32[64,1024]{1,0:T(8,128)S(1)}, u32[]{:S(2)}, u32[]{:S(2)}) collective-permute-start(f32[64,1024]{1,0:T(8,128)} %get-tuple-element.17.refs_0_), channel_id=1, source_target_pairs={{0,4},{1,5},{2,6},{3,7},{4,0},{5,1},{6,2},{7,3},{8,12},{9,13},{10,... | collective-permute-start | bytes 786440 | tf_op jit(solution)/shard_map/ppermute | solution.py:45
  6.7 1.2 collective-permute-start.1
  7.9 8.2 %all-to-all-start = ((f32[8,40,128]{2,1,0:T(8,128)}), f32[8,40,128]{2,1,0:T(8,128)S(1)}, u32[]{:S(2)}, u32[]{:S(2)}) async-start(f32[8,40,128]{2,1,0:T(8,128)} %get-tuple-element.16), calls=%async_computation | async-start | bytes 327680 | tf_op jit(solution)/shard_map/all_to_all | solution.py:350
  16.1 1.5 %collective-permute-start.4 = (f32[64,1024]{1,0:T(8,128)}, f32[64,1024]{1,0:T(8,128)S(1)}, u32[]{:S(2)}, u32[]{:S(2)}) collective-permute-start(f32[64,1024]{1,0:T(8,128)} %get-tuple-element.17.refs_0_), channel_id=1, source_target_pairs={{0,3},{1,0},{2,1},{3,2},{4,7},{5,4},{6,5},{7,6},{8,11},{9,8},{10,9... | collective-permute-start | bytes 786440 | tf_op jit(solution)/shard_map/ppermute | solution.py:37
  17.6 0.0 collective-permute-done.refs_0_.refs_1_
  17.6 1.3 %collective-permute-start.5 = (f32[64,1024]{1,0:T(8,128)S(1)}, f32[64,1024]{1,0:T(8,128)}, u32[]{:S(2)}, u32[]{:S(2)}) collective-permute-start(f32[64,1024]{1,0:T(8,128)S(1)} %collective-permute-done.refs_0_.refs_1_), channel_id=1, source_target_pairs={{0,3},{1,0},{2,1},{3,2},{4,7},{5,4},{6,5},{7,6},{8,11},{9,8},{10,9... | collective-permute-start | bytes 786440 | tf_op jit(solution)/shard_map/ppermute | solution.py:37
  18.8 0.2 collective-permute-start.2
  19.0 0.0 collective-permute-done.1.refs_1_.refs_2_
  19.0 0.1 collective-permute-start.3
  19.1 3.5 %collective-permute-done.4.refs_4_.refs_6_ = f32[64,1024]{1,0:T(8,128)S(1)} collective-permute-done((f32[64,1024]{1,0:T(8,128)}, f32[64,1024]{1,0:T(8,128)S(1)}, u32[]{:S(2)}, u32[]{:S(2)}) %collective-permute-start.4) | collective-permute-done | bytes 262176 | tf_op jit(solution)/shard_map/ppermute | solution.py:37
  22.6 1.9 %all-to-all-done.pieces = f32[8,40,128]{2,1,0:T(8,128)S(1)} async-done(((f32[8,40,128]{2,1,0:T(8,128)}), f32[8,40,128]{2,1,0:T(8,128)S(1)}, u32[]{:S(2)}, u32[]{:S(2)}) %all-to-all-start) | async-done | bytes 163872 | tf_op jit(solution)/shard_map/all_to_all | solution.py:350
  24.5 3.8 %collective-permute-done.5.refs_5_.refs_7_ = f32[64,1024]{1,0:T(8,128)} collective-permute-done((f32[64,1024]{1,0:T(8,128)S(1)}, f32[64,1024]{1,0:T(8,128)}, u32[]{:S(2)}, u32[]{:S(2)}) %collective-permute-start.5) | collective-permute-done | bytes 262176 | tf_op jit(solution)/shard_map/ppermute | solution.py:37
  28.3 0.0 collective-permute-done.2.refs_2_.refs_3_
  28.3 3.1 %collective-permute-done.3.refs_3_.refs_4_ = f32[64,1024]{1,0:T(8,128)S(1)} collective-permute-done((f32[64,1024]{1,0:T(8,128)S(1)}, f32[64,1024]{1,0:T(8,128)S(1)}, u32[]{:S(2)}, u32[]{:S(2)}) %collective-permute-start.3) | collective-permute-done | bytes 262176 | tf_op jit(solution)/shard_map/ppermute | solution.py:37
  31.4 0.0 copy-done.26
  31.4 0.0 copy-done.29
  31.4 0.0 copy-done.27
  31.4 0.0 copy-start.28
  31.4 0.7 copy-done.28
  32.1 2.4 %shard_map.86 = f32[8,80,512]{2,1,0:T(8,128)} custom-call(f32[8,40,128]{2,1,0:T(8,128)} %copy-done.29, f32[64,1024]{1,0:T(8,128)} %copy-done.24, f32[64,1024]{1,0:T(8,128)} %copy-done.25, f32[64,1024]{1,0:T(8,128)} %copy-done.27, f32[64,1024]{1,0:T(8,128)} %copy-done.28, f32[64,1024]{1,0:T(8,128)} %copy-done.26, ...), custom_call_target="tpu_custom_call" | custom-call | bytes 3047424 | tf_op jit(solution)/shard_map/pallas_call | solution.py:60
  34.6 3.7 %all-to-all-start.1 = ((f32[8,80,512]{2,1,0:T(8,128)}), f32[8,80,512]{2,1,0:T(8,128)S(1)}, u32[]{:S(2)}, u32[]{:S(2)}) async-start(f32[8,80,512]{2,1,0:T(8,128)} %shard_map.86), calls=%async_computation.1 | async-start | bytes 2621440 | tf_op jit(solution)/shard_map/all_to_all | solution.py:41
  38.3 1.3 %collective-permute-start.7 = (f32[64,1024]{1,0:T(8,128)S(1)}, f32[64,1024]{1,0:T(8,128)S(1)}, u32[]{:S(2)}, u32[]{:S(2)}) collective-permute-start(f32[64,1024]{1,0:T(8,128)S(1)} %copy-done.5), channel_id=1, source_target_pairs={{0,8},{8,16},{16,24},{24,32},{32,40},{40,48},{48,56},{56,0},{1,9},... | collective-permute-start | bytes 786440 | tf_op jit(solution)/shard_map/ppermute | solution.py:53
  39.5 1.7 %collective-permute-start.10 = (f32[64,1024]{1,0:T(8,128)S(1)}, f32[64,1024]{1,0:T(8,128)S(1)}, u32[]{:S(2)}, u32[]{:S(2)}) collective-permute-start(f32[64,1024]{1,0:T(8,128)S(1)} %copy-done.5), channel_id=1, source_target_pairs={{0,56},{8,0},{16,8},{24,16},{32,24},{40,32},{48,40},{56,48},{1,57}... | collective-permute-start | bytes 786440 | tf_op jit(solution)/shard_map/ppermute | solution.py:53
  41.2 3.7 %collective-permute-done.7.refs_9_.refs_1_ = f32[64,1024]{1,0:T(8,128)S(1)} collective-permute-done((f32[64,1024]{1,0:T(8,128)S(1)}, f32[64,1024]{1,0:T(8,128)S(1)}, u32[]{:S(2)}, u32[]{:S(2)}) %collective-permute-start.7) | collective-permute-done | bytes 262176 | tf_op jit(solution)/shard_map/ppermute | solution.py:53
  44.9 0.0 collective-permute-start.8
  44.9 0.2 collective-permute-done.10.refs_13_.refs_5_
  45.1 2.6 %collective-permute-start.11 = (f32[64,1024]{1,0:T(8,128)S(1)}, f32[64,1024]{1,0:T(8,128)S(1)}, u32[]{:S(2)}, u32[]{:S(2)}) collective-permute-start(f32[64,1024]{1,0:T(8,128)S(1)} %collective-permute-done.10.refs_13_.refs_5_), channel_id=1, source_target_pairs={{0,56},{8,0},{16,8},{24,16},{32,24},{40,32},{48,40},{56,48},{1,57}... | collective-permute-start | bytes 786440 | tf_op jit(solution)/shard_map/ppermute | solution.py:53
  47.6 2.6 %collective-permute-start.6 = (f32[64,1024]{1,0:T(8,128)}, f32[64,1024]{1,0:T(8,128)S(1)}, u32[]{:S(2)}, u32[]{:S(2)}) collective-permute-start(f32[64,1024]{1,0:T(8,128)} %collective-permute-done.5.refs_5_.refs_7_), channel_id=1, source_target_pairs={{0,3},{1,0},{2,1},{3,2},{4,7},{5,4},{6,5},{7,6},{8,11},{9,8},{10,9... | collective-permute-start | bytes 786440 | tf_op jit(solution)/shard_map/ppermute | solution.py:37
  50.2 1.4 %collective-permute-done.8.refs_10_.refs_2_ = f32[64,1024]{1,0:T(8,128)S(1)} collective-permute-done((f32[64,1024]{1,0:T(8,128)S(1)}, f32[64,1024]{1,0:T(8,128)S(1)}, u32[]{:S(2)}, u32[]{:S(2)}) %collective-permute-start.8) | collective-permute-done | bytes 262176 | tf_op jit(solution)/shard_map/ppermute | solution.py:53
  51.6 0.0 collective-permute-start.9
  51.6 0.3 collective-permute-done.11.refs_14_.refs_6_
  51.9 2.5 %collective-permute-start.12 = (f32[64,1024]{1,0:T(8,128)S(1)}, f32[64,1024]{1,0:T(8,128)S(1)}, u32[]{:S(2)}, u32[]{:S(2)}) collective-permute-start(f32[64,1024]{1,0:T(8,128)S(1)} %collective-permute-done.11.refs_14_.refs_6_), channel_id=1, source_target_pairs={{0,56},{8,0},{16,8},{24,16},{32,24},{40,32},{48,40},{56,48},{1,57}... | collective-permute-start | bytes 786440 | tf_op jit(solution)/shard_map/ppermute | solution.py:53
  54.4 0.6 pad_add_fusion.meta
  55.0 2.2 %collective-permute-done.6.refs_5_ = f32[64,1024]{1,0:T(8,128)S(1)} collective-permute-done((f32[64,1024]{1,0:T(8,128)}, f32[64,1024]{1,0:T(8,128)S(1)}, u32[]{:S(2)}, u32[]{:S(2)}) %collective-permute-start.6) | collective-permute-done | bytes 262176 | tf_op jit(solution)/shard_map/ppermute | solution.py:37
  57.2 1.1 all-to-all-done.1.blocks
  58.3 0.0 copy-done.30
  58.3 1.1 copy-done.23
  59.4 2.8 %shard_map.87.refs_0_.refs_8_ = f32[128,1536]{1,0:T(8,128)} custom-call(s32[3]{0:T(128)} %pad_add_fusion.meta, f32[8,80,512]{2,1,0:T(8,128)} %copy-done.23, f32[64,1024]{1,0:T(8,128)} %get-tuple-element.17.refs_0_, f32[64,1024]{1,0:T(8,128)} %copy-done.24, f32[64,1024]{1,0:T(8,128)} %copy-done.25, f32[64,1024]{1,0:T(8,128)} %copy-done.27, ...), custom_call_target="tpu_custom_call" | custom-call | bytes 4194316 | tf_op jit(solution)/shard_map/pallas_call | solution.py:60
  62.3 0.5 collective-permute-start.14
  62.8 0.0 collective-permute-done.9.refs_1_.refs_11_.refs_3_
  62.8 1.2 collective-permute-start.13
  64.0 0.0 collective-permute-done.12.refs_2_.refs_15_.refs_7_
  64.0 0.7 copy-done.17
  64.7 11.7 %shard_map.88 = (bf16[512,512]{1,0:T(8,128)(2,1)}, bf16[512,512]{1,0:T(8,128)(2,1)}, f32[512,1]{1,0:T(8,128)}) custom-call(s32[3]{0:T(128)} %pad_add_fusion.meta, s32[1,512]{1,0:T(1,128)} %order.3, f32[8,80,512]{2,1,0:T(8,128)} %copy-done.23, f32[128,1536]{1,0:T(8,128)} %shard_map.87.refs_0_.refs_8_, f32[64,1024]{1,0:T(8,128)} %copy-done.15, ...), custom_call_target="tpu_custom_call" | custom-call | flops 7247757312 | bytes 3674124 | tf_op jit(solution)/shard_map/pallas_call | solution.py:60
  76.5 0.0 collective-permute-done.13.refs_12_.refs_4_
  76.5 1.6 %collective-permute-done.14.refs_19_.refs_9_ = f32[128,1536]{1,0:T(8,128)S(1)} collective-permute-done((f32[128,1536]{1,0:T(8,128)}, f32[128,1536]{1,0:T(8,128)S(1)}, u32[]{:S(2)}, u32[]{:S(2)}) %collective-permute-start.14) | collective-permute-done | bytes 786464 | tf_op jit(solution)/shard_map/ppermute | solution.py:365
  78.1 0.9 copy-done.3
  79.0 11.0 %shard_map.89 = (f32[64,768]{1,0:T(8,128)}, f32[1024,256]{1,0:T(8,128)}, f32[1024,256]{1,0:T(8,128)}, f32[1024,256]{1,0:T(8,128)}, f32[1024,256]{1,0:T(8,128)}) custom-call(s32[3]{0:T(128)} %pad_add_fusion.meta, s32[1,6]{1,0:T(1,128)} %row_map.1, s32[1,6]{1,0:T(1,128)} %col_map.1, s32[1,512]{1,0:T(1,128)} %order.3, f32[512,1]{1,0:T(8,128)} %get-tuple-element.19.inv, ...), custom_call_target="tpu_custom_call" | custom-call | flops 4227858432 | bytes 13193276 | tf_op jit(solution)/shard_map/pallas_call | solution.py:60
  90.0 4.5 %collective-permute-start.18 = (f32[1024,256]{1,0:T(8,128)}, f32[1024,256]{1,0:T(8,128)S(1)}, u32[]{:S(2)}, u32[]{:S(2)}) collective-permute-start(f32[1024,256]{1,0:T(8,128)} %get-tuple-element.28), channel_id=1, source_target_pairs={{0,64},{64,0},{128,192},{192,128},{1,65},{65,1},{129,193},{193,129... | collective-permute-start | bytes 3145736 | tf_op jit(solution)/shard_map/ppermute | solution.py:391
  94.5 0.1 collective-permute-start.17
  94.6 2.4 %collective-permute-done.18 = f32[1024,256]{1,0:T(8,128)S(1)} collective-permute-done((f32[1024,256]{1,0:T(8,128)}, f32[1024,256]{1,0:T(8,128)S(1)}, u32[]{:S(2)}, u32[]{:S(2)}) %collective-permute-start.18) | collective-permute-done | bytes 1048608 | tf_op jit(solution)/shard_map/ppermute | solution.py:391
  97.1 1.5 %add.6 = f32[1024,256]{1,0:T(8,128)S(1)} add(f32[1024,256]{1,0:T(8,128)} %get-tuple-element.27, f32[1024,256]{1,0:T(8,128)S(1)} %collective-permute-done.18) | non-fusion elementwise | flops 262144 | bytes 3145728 | tf_op jit(solution)/shard_map/add | solution.py:393
  98.6 0.5 collective-permute-start.19
  99.1 0.7 collective-permute-start.15
  99.7 0.0 collective-permute-start.16
  99.7 3.0 %collective-permute-done.15.refs_10_ = f32[128,1536]{1,0:T(8,128)S(1)} collective-permute-done((f32[128,1536]{1,0:T(8,128)S(1)}, f32[128,1536]{1,0:T(8,128)S(1)}, u32[]{:S(2)}, u32[]{:S(2)}) %collective-permute-start.15) | collective-permute-done | bytes 786464 | tf_op jit(solution)/shard_map/ppermute | solution.py:395
  102.7 0.3 collective-permute-done.16.refs_11_
  103.0 0.0 collective-permute-done.17.refs_12_
  103.1 1.1 copy-done.4
  104.2 0.9 copy-done.20
  105.1 15.1 %shard_map.90 = (f32[16,1024]{1,0:T(8,128)}, f32[1024,256]{1,0:T(8,128)S(1)}) custom-call(s32[3]{0:T(128)S(1)} %copy-done.21, s32[1,512]{1,0:T(1,128)S(1)} %bitcast.13, f32[64,1024]{1,0:T(8,128)S(1)} %copy-done.6, f32[64,1024]{1,0:T(8,128)S(1)} %copy-done.8, f32[64,1024]{1,0:T(8,128)S(1)} %copy-done.12, f32[64,1024]{1,0:T(8,128)S(1)} %copy-done.16, ...), custom_call_target="tpu_custom_call" | custom-call | flops 512 | bytes 1024 | tf_op jit(solution)/shard_map/pallas_call | solution.py:60
  120.3 2.7 %collective-permute-done.19 = f32[1024,256]{1,0:T(8,128)S(1)} collective-permute-done((f32[1024,256]{1,0:T(8,128)S(1)}, f32[1024,256]{1,0:T(8,128)S(1)}, u32[]{:S(2)}, u32[]{:S(2)}) %collective-permute-start.19) | collective-permute-done | bytes 1048608 | tf_op jit(solution)/shard_map/ppermute | solution.py:393
  123.0 1.1 add.7
  (51 shorter events, 0.1 us)
Async XLA Ops:
  3.0 14.6 %collective-permute-start = (f32[64,1024]{1,0:T(8,128)}, f32[64,1024]{1,0:T(8,128)S(1)}, u32[]{:S(2)}, u32[]{:S(2)}) collective-permute-start(f32[64,1024]{1,0:T(8,128)} %get-tuple-element.17.refs_0_), channel_id=1, source_target_pairs={{0,4},{1,5},{2,6},{3,7},{4,0},{5,1},{6,2},{7,3},{8,12},{9,13},{10,... | collective-permute-start | bytes 786440 | tf_op jit(solution)/shard_map/ppermute | solution.py:45
  6.7 12.3 %collective-permute-start.1 = (f32[64,1024]{1,0:T(8,128)}, f32[64,1024]{1,0:T(8,128)S(1)}, u32[]{:S(2)}, u32[]{:S(2)}) collective-permute-start(f32[64,1024]{1,0:T(8,128)} %get-tuple-element.17.refs_0_), channel_id=1, source_target_pairs={{0,1},{1,2},{2,3},{3,0},{4,5},{5,6},{6,7},{7,4},{8,9},{9,10},{10,1... | collective-permute-start | bytes 786440 | tf_op jit(solution)/shard_map/ppermute | solution.py:37
  7.9 16.6 %all-to-all-start = ((f32[8,40,128]{2,1,0:T(8,128)}), f32[8,40,128]{2,1,0:T(8,128)S(1)}, u32[]{:S(2)}, u32[]{:S(2)}) async-start(f32[8,40,128]{2,1,0:T(8,128)} %get-tuple-element.16), calls=%async_computation | async-start | bytes 327680 | tf_op jit(solution)/shard_map/all_to_all | solution.py:350
  16.1 6.5 %collective-permute-start.4 = (f32[64,1024]{1,0:T(8,128)}, f32[64,1024]{1,0:T(8,128)S(1)}, u32[]{:S(2)}, u32[]{:S(2)}) collective-permute-start(f32[64,1024]{1,0:T(8,128)} %get-tuple-element.17.refs_0_), channel_id=1, source_target_pairs={{0,3},{1,0},{2,1},{3,2},{4,7},{5,4},{6,5},{7,6},{8,11},{9,8},{10,9... | collective-permute-start | bytes 786440 | tf_op jit(solution)/shard_map/ppermute | solution.py:37
  17.6 13.8 %copy-start.24 = (f32[64,1024]{1,0:T(8,128)}, f32[64,1024]{1,0:T(8,128)S(1)}, u32[]{:S(2)}) copy-start(f32[64,1024]{1,0:T(8,128)S(1)} %collective-permute-done.refs_0_.refs_1_) | copy-start | bytes 786436
  17.6 10.7 %collective-permute-start.5 = (f32[64,1024]{1,0:T(8,128)S(1)}, f32[64,1024]{1,0:T(8,128)}, u32[]{:S(2)}, u32[]{:S(2)}) collective-permute-start(f32[64,1024]{1,0:T(8,128)S(1)} %collective-permute-done.refs_0_.refs_1_), channel_id=1, source_target_pairs={{0,3},{1,0},{2,1},{3,2},{4,7},{5,4},{6,5},{7,6},{8,11},{9,8},{10,9... | collective-permute-start | bytes 786440 | tf_op jit(solution)/shard_map/ppermute | solution.py:37
  18.8 9.5 %collective-permute-start.2 = (f32[64,1024]{1,0:T(8,128)S(1)}, f32[64,1024]{1,0:T(8,128)S(1)}, u32[]{:S(2)}, u32[]{:S(2)}) collective-permute-start(f32[64,1024]{1,0:T(8,128)S(1)} %collective-permute-done.refs_0_.refs_1_), channel_id=1, source_target_pairs={{0,1},{1,2},{2,3},{3,0},{4,5},{5,6},{6,7},{7,4},{8,9},{9,10},{10,1... | collective-permute-start | bytes 786440 | tf_op jit(solution)/shard_map/ppermute | solution.py:37
  19.0 12.4 %copy-start.25 = (f32[64,1024]{1,0:T(8,128)}, f32[64,1024]{1,0:T(8,128)S(1)}, u32[]{:S(2)}) copy-start(f32[64,1024]{1,0:T(8,128)S(1)} %collective-permute-done.1.refs_1_.refs_2_) | copy-start | bytes 786436
  19.0 12.3 %collective-permute-start.3 = (f32[64,1024]{1,0:T(8,128)S(1)}, f32[64,1024]{1,0:T(8,128)S(1)}, u32[]{:S(2)}, u32[]{:S(2)}) collective-permute-start(f32[64,1024]{1,0:T(8,128)S(1)} %collective-permute-done.1.refs_1_.refs_2_), channel_id=1, source_target_pairs={{0,1},{1,2},{2,3},{3,0},{4,5},{5,6},{6,7},{7,4},{8,9},{9,10},{10,1... | collective-permute-start | bytes 786440 | tf_op jit(solution)/shard_map/ppermute | solution.py:37
  22.6 8.8 %copy-start.26 = (f32[64,1024]{1,0:T(8,128)}, f32[64,1024]{1,0:T(8,128)S(1)}, u32[]{:S(2)}) copy-start(f32[64,1024]{1,0:T(8,128)S(1)} %collective-permute-done.4.refs_4_.refs_6_) | copy-start | bytes 786436
  24.5 6.9 %copy-start.29 = (f32[8,40,128]{2,1,0:T(8,128)}, f32[8,40,128]{2,1,0:T(8,128)S(1)}, u32[]{:S(2)}) copy-start(f32[8,40,128]{2,1,0:T(8,128)S(1)} %all-to-all-done.pieces) | copy-start | bytes 491524
  28.3 3.1 %copy-start.27 = (f32[64,1024]{1,0:T(8,128)}, f32[64,1024]{1,0:T(8,128)S(1)}, u32[]{:S(2)}) copy-start(f32[64,1024]{1,0:T(8,128)S(1)} %collective-permute-done.2.refs_2_.refs_3_) | copy-start | bytes 786436
  31.4 0.7 copy-start.28
  34.6 3.7 %copy-start.5 = (f32[64,1024]{1,0:T(8,128)S(1)}, f32[64,1024]{1,0:T(8,128)}, u32[]{:S(2)}) copy-start(f32[64,1024]{1,0:T(8,128)} %get-tuple-element.18.refs_8_.refs_0_) | copy-start | bytes 786436
  34.6 23.8 %all-to-all-start.1 = ((f32[8,80,512]{2,1,0:T(8,128)}), f32[8,80,512]{2,1,0:T(8,128)S(1)}, u32[]{:S(2)}, u32[]{:S(2)}) async-start(f32[8,80,512]{2,1,0:T(8,128)} %shard_map.86), calls=%async_computation.1 | async-start | bytes 2621440 | tf_op jit(solution)/shard_map/all_to_all | solution.py:41
  38.3 6.6 %collective-permute-start.7 = (f32[64,1024]{1,0:T(8,128)S(1)}, f32[64,1024]{1,0:T(8,128)S(1)}, u32[]{:S(2)}, u32[]{:S(2)}) collective-permute-start(f32[64,1024]{1,0:T(8,128)S(1)} %copy-done.5), channel_id=1, source_target_pairs={{0,8},{8,16},{16,24},{24,32},{32,40},{40,48},{48,56},{56,0},{1,9},... | collective-permute-start | bytes 786440 | tf_op jit(solution)/shard_map/ppermute | solution.py:53
  39.5 5.5 %collective-permute-start.10 = (f32[64,1024]{1,0:T(8,128)S(1)}, f32[64,1024]{1,0:T(8,128)S(1)}, u32[]{:S(2)}, u32[]{:S(2)}) collective-permute-start(f32[64,1024]{1,0:T(8,128)S(1)} %copy-done.5), channel_id=1, source_target_pairs={{0,56},{8,0},{16,8},{24,16},{32,24},{40,32},{48,40},{56,48},{1,57}... | collective-permute-start | bytes 786440 | tf_op jit(solution)/shard_map/ppermute | solution.py:53
  44.9 17.4 %copy-start.7 = (f32[64,1024]{1,0:T(8,128)}, f32[64,1024]{1,0:T(8,128)S(1)}, u32[]{:S(2)}) copy-start(f32[64,1024]{1,0:T(8,128)S(1)} %collective-permute-done.7.refs_9_.refs_1_) | copy-start | bytes 786436
  44.9 6.7 %collective-permute-start.8 = (f32[64,1024]{1,0:T(8,128)S(1)}, f32[64,1024]{1,0:T(8,128)S(1)}, u32[]{:S(2)}, u32[]{:S(2)}) collective-permute-start(f32[64,1024]{1,0:T(8,128)S(1)} %collective-permute-done.7.refs_9_.refs_1_), channel_id=1, source_target_pairs={{0,8},{8,16},{16,24},{24,32},{32,40},{40,48},{48,56},{56,0},{1,9},... | collective-permute-start | bytes 786440 | tf_op jit(solution)/shard_map/ppermute | solution.py:53
  45.1 17.2 %copy-start.9 = (f32[64,1024]{1,0:T(8,128)}, f32[64,1024]{1,0:T(8,128)S(1)}, u32[]{:S(2)}) copy-start(f32[64,1024]{1,0:T(8,128)S(1)} %collective-permute-done.10.refs_13_.refs_5_) | copy-start | bytes 786436
  45.1 6.8 %collective-permute-start.11 = (f32[64,1024]{1,0:T(8,128)S(1)}, f32[64,1024]{1,0:T(8,128)S(1)}, u32[]{:S(2)}, u32[]{:S(2)}) collective-permute-start(f32[64,1024]{1,0:T(8,128)S(1)} %collective-permute-done.10.refs_13_.refs_5_), channel_id=1, source_target_pairs={{0,56},{8,0},{16,8},{24,16},{32,24},{40,32},{48,40},{56,48},{1,57}... | collective-permute-start | bytes 786440 | tf_op jit(solution)/shard_map/ppermute | solution.py:53
  47.6 9.6 %collective-permute-start.6 = (f32[64,1024]{1,0:T(8,128)}, f32[64,1024]{1,0:T(8,128)S(1)}, u32[]{:S(2)}, u32[]{:S(2)}) collective-permute-start(f32[64,1024]{1,0:T(8,128)} %collective-permute-done.5.refs_5_.refs_7_), channel_id=1, source_target_pairs={{0,3},{1,0},{2,1},{3,2},{4,7},{5,4},{6,5},{7,6},{8,11},{9,8},{10,9... | collective-permute-start | bytes 786440 | tf_op jit(solution)/shard_map/ppermute | solution.py:37
  51.6 10.7 %copy-start.11 = (f32[64,1024]{1,0:T(8,128)}, f32[64,1024]{1,0:T(8,128)S(1)}, u32[]{:S(2)}) copy-start(f32[64,1024]{1,0:T(8,128)S(1)} %collective-permute-done.8.refs_10_.refs_2_) | copy-start | bytes 786436
  51.6 11.2 %collective-permute-start.9 = (f32[64,1024]{1,0:T(8,128)S(1)}, f32[64,1024]{1,0:T(8,128)S(1)}, u32[]{:S(2)}, u32[]{:S(2)}) collective-permute-start(f32[64,1024]{1,0:T(8,128)S(1)} %collective-permute-done.8.refs_10_.refs_2_), channel_id=1, source_target_pairs={{0,8},{8,16},{16,24},{24,32},{32,40},{40,48},{48,56},{56,0},{1,9},... | collective-permute-start | bytes 786440 | tf_op jit(solution)/shard_map/ppermute | solution.py:53
  51.9 10.4 %copy-start.13 = (f32[64,1024]{1,0:T(8,128)}, f32[64,1024]{1,0:T(8,128)S(1)}, u32[]{:S(2)}) copy-start(f32[64,1024]{1,0:T(8,128)S(1)} %collective-permute-done.11.refs_14_.refs_6_) | copy-start | bytes 786436
  51.9 12.1 %collective-permute-start.12 = (f32[64,1024]{1,0:T(8,128)S(1)}, f32[64,1024]{1,0:T(8,128)S(1)}, u32[]{:S(2)}, u32[]{:S(2)}) collective-permute-start(f32[64,1024]{1,0:T(8,128)S(1)} %collective-permute-done.11.refs_14_.refs_6_), channel_id=1, source_target_pairs={{0,56},{8,0},{16,8},{24,16},{32,24},{40,32},{48,40},{56,48},{1,57}... | collective-permute-start | bytes 786440 | tf_op jit(solution)/shard_map/ppermute | solution.py:53
  57.2 1.1 copy-start.30
  58.3 1.1 copy-start.23
  62.3 15.8 %collective-permute-start.14 = (f32[128,1536]{1,0:T(8,128)}, f32[128,1536]{1,0:T(8,128)S(1)}, u32[]{:S(2)}, u32[]{:S(2)}) collective-permute-start(f32[128,1536]{1,0:T(8,128)} %shard_map.87.refs_0_.refs_8_), channel_id=1, source_target_pairs={{0,128},{64,192},{128,0},{192,64},{1,129},{65,193},{129,1},{193,65... | collective-permute-start | bytes 2359304 | tf_op jit(solution)/shard_map/ppermute | solution.py:365
  62.8 1.2 copy-start.15
  62.8 13.7 %collective-permute-start.13 = (f32[64,1024]{1,0:T(8,128)S(1)}, f32[64,1024]{1,0:T(8,128)S(1)}, u32[]{:S(2)}, u32[]{:S(2)}) collective-permute-start(f32[64,1024]{1,0:T(8,128)S(1)} %collective-permute-done.9.refs_1_.refs_11_.refs_3_), channel_id=1, source_target_pairs={{0,8},{8,16},{16,24},{24,32},{32,40},{40,48},{48,56},{56,0},{1,9},... | collective-permute-start | bytes 786440 | tf_op jit(solution)/shard_map/ppermute | solution.py:53
  64.0 0.7 copy-start.17
  76.5 1.7 %copy-start.19 = (f32[64,1024]{1,0:T(8,128)}, f32[64,1024]{1,0:T(8,128)S(1)}, u32[]{:S(2)}) copy-start(f32[64,1024]{1,0:T(8,128)S(1)} %collective-permute-done.13.refs_12_.refs_4_) | copy-start | bytes 786436
  78.1 0.9 copy-start.3
  79.0 24.0 %copy-start.6 = (f32[64,1024]{1,0:T(8,128)S(1)}, f32[64,1024]{1,0:T(8,128)}, u32[]{:S(2)}) copy-start(f32[64,1024]{1,0:T(8,128)} %get-tuple-element.18.refs_8_.refs_0_) | copy-start | bytes 786436
  79.0 24.0 %copy-start.8 = (f32[64,1024]{1,0:T(8,128)S(1)}, f32[64,1024]{1,0:T(8,128)}, u32[]{:S(2)}) copy-start(f32[64,1024]{1,0:T(8,128)} %copy-done.7) | copy-start | bytes 786436
  79.0 24.0 %copy-start.10 = (f32[64,1024]{1,0:T(8,128)S(1)}, f32[64,1024]{1,0:T(8,128)}, u32[]{:S(2)}) copy-start(f32[64,1024]{1,0:T(8,128)} %copy-done.9) | copy-start | bytes 786436
  79.0 24.0 %copy-start.12 = (f32[64,1024]{1,0:T(8,128)S(1)}, f32[64,1024]{1,0:T(8,128)}, u32[]{:S(2)}) copy-start(f32[64,1024]{1,0:T(8,128)} %copy-done.11) | copy-start | bytes 786436
  79.0 24.0 %copy-start.14 = (f32[64,1024]{1,0:T(8,128)S(1)}, f32[64,1024]{1,0:T(8,128)}, u32[]{:S(2)}) copy-start(f32[64,1024]{1,0:T(8,128)} %copy-done.13) | copy-start | bytes 786436
  79.0 24.0 %copy-start.16 = (f32[64,1024]{1,0:T(8,128)S(1)}, f32[64,1024]{1,0:T(8,128)}, u32[]{:S(2)}) copy-start(f32[64,1024]{1,0:T(8,128)} %copy-done.15) | copy-start | bytes 786436
  79.0 24.0 %copy-start.18 = (f32[64,1024]{1,0:T(8,128)S(1)}, f32[64,1024]{1,0:T(8,128)}, u32[]{:S(2)}) copy-start(f32[64,1024]{1,0:T(8,128)} %copy-done.17) | copy-start | bytes 786436
  90.0 7.0 %collective-permute-start.18 = (f32[1024,256]{1,0:T(8,128)}, f32[1024,256]{1,0:T(8,128)S(1)}, u32[]{:S(2)}, u32[]{:S(2)}) collective-permute-start(f32[1024,256]{1,0:T(8,128)} %get-tuple-element.28), channel_id=1, source_target_pairs={{0,64},{64,0},{128,192},{192,128},{1,65},{65,1},{129,193},{193,129... | collective-permute-start | bytes 3145736 | tf_op jit(solution)/shard_map/ppermute | solution.py:391
  94.5 8.4 %collective-permute-start.17 = (f32[1024,256]{1,0:T(8,128)}, f32[1024,256]{1,0:T(8,128)S(1)}, u32[]{:S(2)}, u32[]{:S(2)}) collective-permute-start(f32[1024,256]{1,0:T(8,128)} %get-tuple-element.23), channel_id=1, source_target_pairs={{0,64},{64,0},{128,192},{192,128},{1,65},{65,1},{129,193},{193,129... | collective-permute-start | bytes 3145736 | tf_op jit(solution)/shard_map/ppermute | solution.py:392
  97.0 2.0 %copy-start.1 = (f32[128,1536]{1,0:T(8,128)S(1)}, f32[128,1536]{1,0:T(8,128)}, u32[]{:S(2)}) copy-start(f32[128,1536]{1,0:T(8,128)} %shard_map.87.refs_0_.refs_8_) | copy-start | bytes 2359300
  97.0 6.0 %copy-start = (f32[1088,272]{0,1:T(8,128)S(1)}, f32[1088,272]{0,1:T(8,128)}, u32[]{:S(2)}) copy-start(f32[1088,272]{0,1:T(8,128)} %param.8) | copy-start | bytes 3551236
  97.0 6.0 %copy-start.2 = (f32[1024,256]{1,0:T(8,128)S(1)}, f32[1024,256]{1,0:T(8,128)}, u32[]{:S(2)}) copy-start(f32[1024,256]{1,0:T(8,128)} %get-tuple-element.24.refs_13_) | copy-start | bytes 3145732
  97.0 6.0 %copy-start.21 = (s32[3]{0:T(128)S(1)}, s32[3]{0:T(128)}, u32[]{:S(2)}) copy-start(s32[3]{0:T(128)} %pad_add_fusion.meta) | copy-start | bytes 40
  97.0 6.0 %copy-start.22 = (s32[512]{0:T(512)S(1)}, s32[512]{0:T(512)}, u32[]{:S(2)}) copy-start(s32[512]{0:T(512)} %param.9) | copy-start | bytes 6148
  98.6 24.5 %collective-permute-start.19 = (f32[1024,256]{1,0:T(8,128)S(1)}, f32[1024,256]{1,0:T(8,128)S(1)}, u32[]{:S(2)}, u32[]{:S(2)}) collective-permute-start(f32[1024,256]{1,0:T(8,128)S(1)} %add.6), channel_id=1, source_target_pairs={{0,128},{64,192},{128,0},{192,64},{1,129},{65,193},{129,1},{193,65... | collective-permute-start | bytes 3145736 | tf_op jit(solution)/shard_map/ppermute | solution.py:393
  99.1 3.7 %collective-permute-start.15 = (f32[128,1536]{1,0:T(8,128)S(1)}, f32[128,1536]{1,0:T(8,128)S(1)}, u32[]{:S(2)}, u32[]{:S(2)}) collective-permute-start(f32[128,1536]{1,0:T(8,128)S(1)} %copy-done.1), channel_id=1, source_target_pairs={{0,64},{64,0},{128,192},{192,128},{1,65},{65,1},{129,193},{193,129... | collective-permute-start | bytes 2359304 | tf_op jit(solution)/shard_map/ppermute | solution.py:395
  99.7 3.2 %collective-permute-start.16 = (f32[128,1536]{1,0:T(8,128)}, f32[128,1536]{1,0:T(8,128)S(1)}, u32[]{:S(2)}, u32[]{:S(2)}) collective-permute-start(f32[128,1536]{1,0:T(8,128)} %copy-done.3), channel_id=1, source_target_pairs={{0,64},{64,0},{128,192},{192,128},{1,65},{65,1},{129,193},{193,129... | collective-permute-start | bytes 2359304 | tf_op jit(solution)/shard_map/ppermute | solution.py:395
  103.1 1.1 copy-start.4
  104.2 0.9 copy-start.20

commit v3 on v2

--- a/solution.py
+++ b/solution.py
@@ -90,7 +90,7 @@
     rest = value - first.astype(F32)
     second = rest.astype(BF16)
     third = (rest - second.astype(F32)).astype(BF16)
-    return mm(hot, first) + (mm(hot, second) + mm(hot, third))
+    return mm(jnp.concatenate([hot, hot, hot], 1), jnp.concatenate([first, second, third], 0))
 
 
 def hot_rows(order, meta, held):
@@ -128,15 +128,19 @@
     tf[...] = total
     th[...], tl[...] = split(total)
 
-    @pl.loop(0, 4)
+    ph[...], pw[...] = split(mm3(ph[...], pw[...], ph[...], pw[...]))
+
+    @pl.loop(0, 3)
     def _(_):
-        h, w = split(mm3(ph[...], pw[...], ph[...], pw[...]))
-        ph[...] = h
-        pw[...] = w
-        new = tf[...] + mm3(ph[...], pw[...], th[...], tl[...])
+        high = jnp.concatenate([ph[...], th[...]], 1)
+        low = jnp.concatenate([pw[...], tl[...]], 1)
+        both = mm3(ph[...], pw[...], high, low)
+        ph[...], pw[...] = split(both[:, :PB])
+        new = tf[...] + both[:, PB:]
         tf[...] = new
         th[...], tl[...] = split(new)
 
+    th[...], tl[...] = split(tf[...] + mm3(ph[...], pw[...], th[...], tl[...]))
     return inv_diag
 
 
@@ -351,7 +355,12 @@
     left_parts = pcol_steps(left_t)
     ties = [left_parts[i] for i in (1, 2, 3, 4, 6, 7)]
     (panel,) = call(
-        mid_kernel, [sds(8, N + PP, PB)], [pieces] + ties, parts=len(ties)
+        mid_kernel,
+        [sds(8, N + PP, PB)],
+        [pieces] + ties,
+        parts=len(ties),
+        limit=16,
+        where=HBM,
     )
     panel = pcol_gather(panel)
     (parent_one,) = call(

time: 125 us -> 123 us (0.984)
  local copies, waits for them, and re-layouts: 5.6 us -> 3.81 us
  Pallas kernels: 45.4 us -> 43.9 us
    unnamed x62 -> x60, local copies, waits for them, and re-layouts: 5.6 us -> 3.81 us
    pallas_call x5, Pallas kernels: 43.1 us -> 41.6 us  [call(): pl.pallas_call(kernel, out_shape=tuple(outs), in_specs=[SMEM] * smem + [V...]
where the time goes in v3:
time: 123 us; the launch traced here: 122 us
  Pallas kernels  43.9 us (36%)
  starting transfers between devices  38 us (31%)
  waiting for transfers between devices  32.3 us (26%)
  local copies, waits for them, and re-layouts  3.81 us (3%)
  other arithmetic  3.2 us (3%)
    pallas_call x5, Pallas kernels, call(): pl.pallas_call(kernel, out_shape=tuple(outs), in_specs=[SMEM] * smem + [V...  41.6 us
    ppermute x6, waiting for transfers between devices, x_step(): return lax.ppermute(value, 'pcol', pairs)  12.7 us
    ppermute x7, starting transfers between devices, z_step(): return lax.ppermute(value, 'prow', [(i, (i + step) % 8) for i in range(8)])  8.76 us
    all_to_all x1, starting transfers between devices, body(): pieces = lax.all_to_all(piece, 'prow', 0, 0, tiled=True)  8.19 us
    ppermute x6, starting transfers between devices, x_step(): return lax.ppermute(value, 'pcol', pairs)  6.7 us
    ppermute x7, waiting for transfers between devices, z_step(): return lax.ppermute(value, 'prow', [(i, (i + step) % 8) for i in range(8)])  6.08 us
    ppermute x1, starting transfers between devices, body(): over = core_flip(terms[3])  4.42 us
    all_to_all x1, starting transfers between devices, pcol_gather(): return lax.all_to_all(copies, 'pcol', 0, 0, tiled=True)  4.41 us
  transfers between devices with their start and end apart: 22, of which 15 were waited for; matrix products, arithmetic and copies ran while one was open for 2% of the time, Pallas kernels for 24%

profile of v3, /device:TPU:1, one launch (start us, length us, event | category | flops | bytes accessed | tf_op | source)
XLA Modules:
  0.0 122.1 jit_solution(12603245896748388764)
XLA Ops:
  0.6 2.3 %shard_map.85 = (f32[8,40,128]{2,1,0:T(8,128)}, f32[64,1024]{1,0:T(8,128)}, f32[64,1024]{1,0:T(8,128)}) custom-call(f32[832,832]{1,0:T(8,128)} %bitcast.14, f32[832,832]{1,0:T(8,128)} %bitcast.15, f32[272,1088]{1,0:T(8,128)} %bitcast.10, f32[272,1088]{1,0:T(8,128)} %bitcast.11), custom_call_target="tpu_custom_call" | custom-call | tf_op jit(solution)/shard_map/pallas_call | solution.py:168
  2.9 3.7 %collective-permute-start = (f32[64,1024]{1,0:T(8,128)}, f32[64,1024]{1,0:T(8,128)S(1)}, u32[]{:S(2)}, u32[]{:S(2)}) collective-permute-start(f32[64,1024]{1,0:T(8,128)} %get-tuple-element.17.refs_0_), channel_id=1, source_target_pairs={{0,4},{1,5},{2,6},{3,7},{4,0},{5,1},{6,2},{7,3},{8,12},{9,13},{10,... | collective-permute-start | bytes 786440 | tf_op jit(solution)/shard_map/ppermute | solution.py:45
  6.7 1.2 collective-permute-start.1
  7.9 8.2 %all-to-all-start = ((f32[8,40,128]{2,1,0:T(8,128)}), f32[8,40,128]{2,1,0:T(8,128)S(1)}, u32[]{:S(2)}, u32[]{:S(2)}) async-start(f32[8,40,128]{2,1,0:T(8,128)} %get-tuple-element.16), calls=%async_computation | async-start | bytes 327680 | tf_op jit(solution)/shard_map/all_to_all | solution.py:354
  16.1 1.5 %collective-permute-start.4 = (f32[64,1024]{1,0:T(8,128)}, f32[64,1024]{1,0:T(8,128)S(1)}, u32[]{:S(2)}, u32[]{:S(2)}) collective-permute-start(f32[64,1024]{1,0:T(8,128)} %get-tuple-element.17.refs_0_), channel_id=1, source_target_pairs={{0,3},{1,0},{2,1},{3,2},{4,7},{5,4},{6,5},{7,6},{8,11},{9,8},{10,9... | collective-permute-start | bytes 786440 | tf_op jit(solution)/shard_map/ppermute | solution.py:37
  17.5 0.0 collective-permute-done.refs_0_.refs_1_
  17.6 1.3 %collective-permute-start.5 = (f32[64,1024]{1,0:T(8,128)S(1)}, f32[64,1024]{1,0:T(8,128)S(1)}, u32[]{:S(2)}, u32[]{:S(2)}) collective-permute-start(f32[64,1024]{1,0:T(8,128)S(1)} %collective-permute-done.refs_0_.refs_1_), channel_id=1, source_target_pairs={{0,3},{1,0},{2,1},{3,2},{4,7},{5,4},{6,5},{7,6},{8,11},{9,8},{10,9... | collective-permute-start | bytes 786440 | tf_op jit(solution)/shard_map/ppermute | solution.py:37
  18.8 0.2 collective-permute-start.2
  19.0 0.0 collective-permute-done.1.refs_1_.refs_2_
  19.0 0.1 collective-permute-start.3
  19.1 3.5 %collective-permute-done.4.refs_4_.refs_6_ = f32[64,1024]{1,0:T(8,128)S(1)} collective-permute-done((f32[64,1024]{1,0:T(8,128)}, f32[64,1024]{1,0:T(8,128)S(1)}, u32[]{:S(2)}, u32[]{:S(2)}) %collective-permute-start.4) | collective-permute-done | bytes 262176 | tf_op jit(solution)/shard_map/ppermute | solution.py:37
  22.6 1.9 %all-to-all-done.pieces = f32[8,40,128]{2,1,0:T(8,128)S(1)} async-done(((f32[8,40,128]{2,1,0:T(8,128)}), f32[8,40,128]{2,1,0:T(8,128)S(1)}, u32[]{:S(2)}, u32[]{:S(2)}) %all-to-all-start) | async-done | bytes 163872 | tf_op jit(solution)/shard_map/all_to_all | solution.py:354
  24.4 3.7 %collective-permute-done.5.refs_5_.refs_7_ = f32[64,1024]{1,0:T(8,128)S(1)} collective-permute-done((f32[64,1024]{1,0:T(8,128)S(1)}, f32[64,1024]{1,0:T(8,128)S(1)}, u32[]{:S(2)}, u32[]{:S(2)}) %collective-permute-start.5) | collective-permute-done | bytes 262176 | tf_op jit(solution)/shard_map/ppermute | solution.py:37
  28.2 0.0 collective-permute-done.2.refs_2_.refs_3_
  28.2 3.2 %collective-permute-done.3.refs_3_.refs_4_ = f32[64,1024]{1,0:T(8,128)S(1)} collective-permute-done((f32[64,1024]{1,0:T(8,128)S(1)}, f32[64,1024]{1,0:T(8,128)S(1)}, u32[]{:S(2)}, u32[]{:S(2)}) %collective-permute-start.3) | collective-permute-done | bytes 262176 | tf_op jit(solution)/shard_map/ppermute | solution.py:37
  31.4 1.5 %shard_map.86 = f32[8,80,512]{2,1,0:T(8,128)} custom-call(f32[8,40,128]{2,1,0:T(8,128)S(1)} %all-to-all-done.pieces, f32[64,1024]{1,0:T(8,128)S(1)} %collective-permute-done.refs_0_.refs_1_, f32[64,1024]{1,0:T(8,128)S(1)} %collective-permute-done.1.refs_1_.refs_2_, f32[64,1024]{1,0:T(8,128)S(1)} %collective-permute-done.2.refs_2_.refs_3_, ...), custom_call_target="tpu_custom_call" | custom-call | bytes 3047424 | tf_op jit(solution)/shard_map/pallas_call | solution.py:60
  32.9 0.0 copy-done.2
  32.9 0.0 copy-done.3
  32.9 0.0 copy-done.4
  32.9 4.4 %all-to-all-start.1 = ((f32[8,80,512]{2,1,0:T(8,128)}), f32[8,80,512]{2,1,0:T(8,128)}, u32[]{:S(2)}, u32[]{:S(2)}) async-start(f32[8,80,512]{2,1,0:T(8,128)} %shard_map.86), calls=%async_computation.1 | async-start | bytes 2621440 | tf_op jit(solution)/shard_map/all_to_all | solution.py:41
  37.3 1.3 %collective-permute-start.7 = (f32[64,1024]{1,0:T(8,128)S(1)}, f32[64,1024]{1,0:T(8,128)S(1)}, u32[]{:S(2)}, u32[]{:S(2)}) collective-permute-start(f32[64,1024]{1,0:T(8,128)S(1)} %copy-done.11), channel_id=1, source_target_pairs={{0,8},{8,16},{16,24},{24,32},{32,40},{40,48},{48,56},{56,0},{1,9},... | collective-permute-start | bytes 786440 | tf_op jit(solution)/shard_map/ppermute | solution.py:53
  38.6 1.5 %collective-permute-start.10 = (f32[64,1024]{1,0:T(8,128)S(1)}, f32[64,1024]{1,0:T(8,128)S(1)}, u32[]{:S(2)}, u32[]{:S(2)}) collective-permute-start(f32[64,1024]{1,0:T(8,128)S(1)} %copy-done.11), channel_id=1, source_target_pairs={{0,56},{8,0},{16,8},{24,16},{32,24},{40,32},{48,40},{56,48},{1,57}... | collective-permute-start | bytes 786440 | tf_op jit(solution)/shard_map/ppermute | solution.py:53
  40.1 3.8 %collective-permute-done.7.refs_9_.refs_1_ = f32[64,1024]{1,0:T(8,128)S(1)} collective-permute-done((f32[64,1024]{1,0:T(8,128)S(1)}, f32[64,1024]{1,0:T(8,128)S(1)}, u32[]{:S(2)}, u32[]{:S(2)}) %collective-permute-start.7) | collective-permute-done | bytes 262176 | tf_op jit(solution)/shard_map/ppermute | solution.py:53
  43.8 0.0 collective-permute-start.8
  43.8 0.4 collective-permute-done.10.refs_13_.refs_5_
  44.2 2.3 %collective-permute-start.11 = (f32[64,1024]{1,0:T(8,128)S(1)}, f32[64,1024]{1,0:T(8,128)S(1)}, u32[]{:S(2)}, u32[]{:S(2)}) collective-permute-start(f32[64,1024]{1,0:T(8,128)S(1)} %collective-permute-done.10.refs_13_.refs_5_), channel_id=1, source_target_pairs={{0,56},{8,0},{16,8},{24,16},{32,24},{40,32},{48,40},{56,48},{1,57}... | collective-permute-start | bytes 786440 | tf_op jit(solution)/shard_map/ppermute | solution.py:53
  46.5 2.5 %collective-permute-start.6 = (f32[64,1024]{1,0:T(8,128)S(1)}, f32[64,1024]{1,0:T(8,128)S(1)}, u32[]{:S(2)}, u32[]{:S(2)}) collective-permute-start(f32[64,1024]{1,0:T(8,128)S(1)} %collective-permute-done.5.refs_5_.refs_7_), channel_id=1, source_target_pairs={{0,3},{1,0},{2,1},{3,2},{4,7},{5,4},{6,5},{7,6},{8,11},{9,8},{10,9... | collective-permute-start | bytes 786440 | tf_op jit(solution)/shard_map/ppermute | solution.py:37
  49.0 1.7 %collective-permute-done.8.refs_10_.refs_2_ = f32[64,1024]{1,0:T(8,128)S(1)} collective-permute-done((f32[64,1024]{1,0:T(8,128)S(1)}, f32[64,1024]{1,0:T(8,128)S(1)}, u32[]{:S(2)}, u32[]{:S(2)}) %collective-permute-start.8) | collective-permute-done | bytes 262176 | tf_op jit(solution)/shard_map/ppermute | solution.py:53
  50.7 0.1 collective-permute-start.9
  50.8 0.3 collective-permute-done.11.refs_14_.refs_6_
  51.0 2.4 %collective-permute-start.12 = (f32[64,1024]{1,0:T(8,128)S(1)}, f32[64,1024]{1,0:T(8,128)S(1)}, u32[]{:S(2)}, u32[]{:S(2)}) collective-permute-start(f32[64,1024]{1,0:T(8,128)S(1)} %collective-permute-done.11.refs_14_.refs_6_), channel_id=1, source_target_pairs={{0,56},{8,0},{16,8},{24,16},{32,24},{40,32},{48,40},{56,48},{1,57}... | collective-permute-start | bytes 786440 | tf_op jit(solution)/shard_map/ppermute | solution.py:53
  53.5 0.6 pad_add_fusion.meta
  54.1 2.3 %collective-permute-done.6.refs_5_ = f32[64,1024]{1,0:T(8,128)S(1)} collective-permute-done((f32[64,1024]{1,0:T(8,128)S(1)}, f32[64,1024]{1,0:T(8,128)S(1)}, u32[]{:S(2)}, u32[]{:S(2)}) %collective-permute-start.6) | collective-permute-done | bytes 262176 | tf_op jit(solution)/shard_map/ppermute | solution.py:37
  56.3 1.1 all-to-all-done.1.blocks
  57.5 2.8 %shard_map.87.refs_0_.refs_8_ = f32[128,1536]{1,0:T(8,128)} custom-call(s32[3]{0:T(128)} %pad_add_fusion.meta, f32[8,80,512]{2,1,0:T(8,128)} %all-to-all-done.1.blocks, f32[64,1024]{1,0:T(8,128)} %get-tuple-element.17.refs_0_, f32[64,1024]{1,0:T(8,128)} %copy-done.2, f32[64,1024]{1,0:T(8,128)} %copy-done.3, f32[64,1024]{1,0:T(8,128)} %copy-done.6, ...), custom_call_target="tpu_custom_call" | custom-call | bytes 4194316 | tf_op jit(solution)/shard_map/pallas_call | solution.py:60
  60.3 0.5 collective-permute-start.14
  60.8 0.0 collective-permute-done.9.refs_1_.refs_11_.refs_3_
  60.8 1.2 collective-permute-start.13
  62.0 0.0 collective-permute-done.12.refs_2_.refs_15_.refs_7_
  62.0 0.7 copy-done.23
  62.7 11.6 %shard_map.88 = (bf16[512,512]{1,0:T(8,128)(2,1)}, bf16[512,512]{1,0:T(8,128)(2,1)}, f32[512,1]{1,0:T(8,128)}) custom-call(s32[3]{0:T(128)} %pad_add_fusion.meta, s32[1,512]{1,0:T(1,128)} %order.3, f32[8,80,512]{2,1,0:T(8,128)} %all-to-all-done.1.blocks, f32[128,1536]{1,0:T(8,128)} %shard_map.87.refs_0_.refs_8_, f32[64,1024]{1,0:T(8,128)} %copy-done.21, ...), custom_call_target="tpu_custom_call" | custom-call | flops 7247757312 | bytes 3674124 | tf_op jit(solution)/shard_map/pallas_call | solution.py:60
  74.4 0.0 collective-permute-done.13.refs_12_.refs_4_
  74.4 1.8 %collective-permute-done.14.refs_19_.refs_9_ = f32[128,1536]{1,0:T(8,128)S(1)} collective-permute-done((f32[128,1536]{1,0:T(8,128)}, f32[128,1536]{1,0:T(8,128)S(1)}, u32[]{:S(2)}, u32[]{:S(2)}) %collective-permute-start.14) | collective-permute-done | bytes 786464 | tf_op jit(solution)/shard_map/ppermute | solution.py:374
  76.2 0.9 copy-done.9
  77.1 0.0 copy-start.20
  77.2 0.0 copy-start.22
  77.2 0.0 copy-start.24
  77.2 10.9 %shard_map.89 = (f32[64,768]{1,0:T(8,128)}, f32[1024,256]{1,0:T(8,128)}, f32[1024,256]{1,0:T(8,128)}, f32[1024,256]{1,0:T(8,128)}, f32[1024,256]{1,0:T(8,128)}) custom-call(s32[3]{0:T(128)} %pad_add_fusion.meta, s32[1,6]{1,0:T(1,128)} %row_map.1, s32[1,6]{1,0:T(1,128)} %col_map.1, s32[1,512]{1,0:T(1,128)} %order.3, f32[512,1]{1,0:T(8,128)} %get-tuple-element.19.inv, ...), custom_call_target="tpu_custom_call" | custom-call | flops 4227858432 | bytes 13193276 | tf_op jit(solution)/shard_map/pallas_call | solution.py:60
  88.1 4.4 %collective-permute-start.18 = (f32[1024,256]{1,0:T(8,128)}, f32[1024,256]{1,0:T(8,128)S(1)}, u32[]{:S(2)}, u32[]{:S(2)}) collective-permute-start(f32[1024,256]{1,0:T(8,128)} %get-tuple-element.28), channel_id=1, source_target_pairs={{0,64},{64,0},{128,192},{192,128},{1,65},{65,1},{129,193},{193,129... | collective-permute-start | bytes 3145736 | tf_op jit(solution)/shard_map/ppermute | solution.py:400
  92.5 0.1 collective-permute-start.17
  92.6 2.4 %collective-permute-done.18 = f32[1024,256]{1,0:T(8,128)S(1)} collective-permute-done((f32[1024,256]{1,0:T(8,128)}, f32[1024,256]{1,0:T(8,128)S(1)}, u32[]{:S(2)}, u32[]{:S(2)}) %collective-permute-start.18) | collective-permute-done | bytes 1048608 | tf_op jit(solution)/shard_map/ppermute | solution.py:400
  95.0 1.5 %add.6 = f32[1024,256]{1,0:T(8,128)S(1)} add(f32[1024,256]{1,0:T(8,128)} %get-tuple-element.27, f32[1024,256]{1,0:T(8,128)S(1)} %collective-permute-done.18) | non-fusion elementwise | flops 262144 | bytes 3145728 | tf_op jit(solution)/shard_map/add | solution.py:402
  96.5 0.5 collective-permute-start.19
  97.0 0.7 collective-permute-start.15
  97.7 0.0 collective-permute-start.16
  97.7 3.0 %collective-permute-done.15.refs_10_ = f32[128,1536]{1,0:T(8,128)S(1)} collective-permute-done((f32[128,1536]{1,0:T(8,128)S(1)}, f32[128,1536]{1,0:T(8,128)S(1)}, u32[]{:S(2)}, u32[]{:S(2)}) %collective-permute-start.15) | collective-permute-done | bytes 786464 | tf_op jit(solution)/shard_map/ppermute | solution.py:404
  100.7 0.3 collective-permute-done.16.refs_11_
  100.9 0.0 collective-permute-done.17.refs_12_
  100.9 0.0 copy-done.16
  101.0 1.1 copy-done.10
  102.2 0.9 copy-done.26
  103.1 14.8 %shard_map.90 = (f32[16,1024]{1,0:T(8,128)}, f32[1024,256]{1,0:T(8,128)S(1)}) custom-call(s32[3]{0:T(128)S(1)} %copy-done.27, s32[1,512]{1,0:T(1,128)S(1)} %bitcast.13, f32[64,1024]{1,0:T(8,128)S(1)} %copy-done.12, f32[64,1024]{1,0:T(8,128)S(1)} %copy-done.14, f32[64,1024]{1,0:T(8,128)S(1)} %copy-done.18, f32[64,1024]{1,0:T(8,128)S(1)} %copy-done.22, ...), custom_call_target="tpu_custom_call" | custom-call | flops 512 | bytes 1024 | tf_op jit(solution)/shard_map/pallas_call | solution.py:60
  117.9 3.1 %collective-permute-done.19 = f32[1024,256]{1,0:T(8,128)S(1)} collective-permute-done((f32[1024,256]{1,0:T(8,128)S(1)}, f32[1024,256]{1,0:T(8,128)S(1)}, u32[]{:S(2)}, u32[]{:S(2)}) %collective-permute-start.19) | collective-permute-done | bytes 1048608 | tf_op jit(solution)/shard_map/ppermute | solution.py:402
  121.0 1.1 add.7
  (49 shorter events, 0.1 us)
Async XLA Ops:
  2.9 14.6 %collective-permute-start = (f32[64,1024]{1,0:T(8,128)}, f32[64,1024]{1,0:T(8,128)S(1)}, u32[]{:S(2)}, u32[]{:S(2)}) collective-permute-start(f32[64,1024]{1,0:T(8,128)} %get-tuple-element.17.refs_0_), channel_id=1, source_target_pairs={{0,4},{1,5},{2,6},{3,7},{4,0},{5,1},{6,2},{7,3},{8,12},{9,13},{10,... | collective-permute-start | bytes 786440 | tf_op jit(solution)/shard_map/ppermute | solution.py:45
  6.7 12.3 %collective-permute-start.1 = (f32[64,1024]{1,0:T(8,128)}, f32[64,1024]{1,0:T(8,128)S(1)}, u32[]{:S(2)}, u32[]{:S(2)}) collective-permute-start(f32[64,1024]{1,0:T(8,128)} %get-tuple-element.17.refs_0_), channel_id=1, source_target_pairs={{0,1},{1,2},{2,3},{3,0},{4,5},{5,6},{6,7},{7,4},{8,9},{9,10},{10,1... | collective-permute-start | bytes 786440 | tf_op jit(solution)/shard_map/ppermute | solution.py:37
  7.9 16.6 %all-to-all-start = ((f32[8,40,128]{2,1,0:T(8,128)}), f32[8,40,128]{2,1,0:T(8,128)S(1)}, u32[]{:S(2)}, u32[]{:S(2)}) async-start(f32[8,40,128]{2,1,0:T(8,128)} %get-tuple-element.16), calls=%async_computation | async-start | bytes 327680 | tf_op jit(solution)/shard_map/all_to_all | solution.py:354
  16.1 6.5 %collective-permute-start.4 = (f32[64,1024]{1,0:T(8,128)}, f32[64,1024]{1,0:T(8,128)S(1)}, u32[]{:S(2)}, u32[]{:S(2)}) collective-permute-start(f32[64,1024]{1,0:T(8,128)} %get-tuple-element.17.refs_0_), channel_id=1, source_target_pairs={{0,3},{1,0},{2,1},{3,2},{4,7},{5,4},{6,5},{7,6},{8,11},{9,8},{10,9... | collective-permute-start | bytes 786440 | tf_op jit(solution)/shard_map/ppermute | solution.py:37
  17.5 15.3 %copy-start.2 = (f32[64,1024]{1,0:T(8,128)}, f32[64,1024]{1,0:T(8,128)S(1)}, u32[]{:S(2)}) copy-start(f32[64,1024]{1,0:T(8,128)S(1)} %collective-permute-done.refs_0_.refs_1_) | copy-start | bytes 786436
  17.6 10.6 %collective-permute-start.5 = (f32[64,1024]{1,0:T(8,128)S(1)}, f32[64,1024]{1,0:T(8,128)S(1)}, u32[]{:S(2)}, u32[]{:S(2)}) collective-permute-start(f32[64,1024]{1,0:T(8,128)S(1)} %collective-permute-done.refs_0_.refs_1_), channel_id=1, source_target_pairs={{0,3},{1,0},{2,1},{3,2},{4,7},{5,4},{6,5},{7,6},{8,11},{9,8},{10,9... | collective-permute-start | bytes 786440 | tf_op jit(solution)/shard_map/ppermute | solution.py:37
  18.8 9.4 %collective-permute-start.2 = (f32[64,1024]{1,0:T(8,128)S(1)}, f32[64,1024]{1,0:T(8,128)S(1)}, u32[]{:S(2)}, u32[]{:S(2)}) collective-permute-start(f32[64,1024]{1,0:T(8,128)S(1)} %collective-permute-done.refs_0_.refs_1_), channel_id=1, source_target_pairs={{0,1},{1,2},{2,3},{3,0},{4,5},{5,6},{6,7},{7,4},{8,9},{9,10},{10,1... | collective-permute-start | bytes 786440 | tf_op jit(solution)/shard_map/ppermute | solution.py:37
  19.0 13.8 %copy-start.3 = (f32[64,1024]{1,0:T(8,128)}, f32[64,1024]{1,0:T(8,128)S(1)}, u32[]{:S(2)}) copy-start(f32[64,1024]{1,0:T(8,128)S(1)} %collective-permute-done.1.refs_1_.refs_2_) | copy-start | bytes 786436
  19.0 12.3 %collective-permute-start.3 = (f32[64,1024]{1,0:T(8,128)S(1)}, f32[64,1024]{1,0:T(8,128)S(1)}, u32[]{:S(2)}, u32[]{:S(2)}) collective-permute-start(f32[64,1024]{1,0:T(8,128)S(1)} %collective-permute-done.1.refs_1_.refs_2_), channel_id=1, source_target_pairs={{0,1},{1,2},{2,3},{3,0},{4,5},{5,6},{6,7},{7,4},{8,9},{9,10},{10,1... | collective-permute-start | bytes 786440 | tf_op jit(solution)/shard_map/ppermute | solution.py:37
  22.6 10.3 %copy-start.4 = (f32[64,1024]{1,0:T(8,128)}, f32[64,1024]{1,0:T(8,128)S(1)}, u32[]{:S(2)}) copy-start(f32[64,1024]{1,0:T(8,128)S(1)} %collective-permute-done.4.refs_4_.refs_6_) | copy-start | bytes 786436
  28.2 18.3 %copy-start.5 = (f32[64,1024]{1,0:T(8,128)}, f32[64,1024]{1,0:T(8,128)S(1)}, u32[]{:S(2)}) copy-start(f32[64,1024]{1,0:T(8,128)S(1)} %collective-permute-done.5.refs_5_.refs_7_) | copy-start | bytes 786436
  28.2 4.7 %copy-start.6 = (f32[64,1024]{1,0:T(8,128)}, f32[64,1024]{1,0:T(8,128)S(1)}, u32[]{:S(2)}) copy-start(f32[64,1024]{1,0:T(8,128)S(1)} %collective-permute-done.2.refs_2_.refs_3_) | copy-start | bytes 786436
  31.4 1.5 %copy-start.7 = (f32[64,1024]{1,0:T(8,128)}, f32[64,1024]{1,0:T(8,128)S(1)}, u32[]{:S(2)}) copy-start(f32[64,1024]{1,0:T(8,128)S(1)} %collective-permute-done.3.refs_3_.refs_4_) | copy-start | bytes 786436
  32.9 4.4 %copy-start.11 = (f32[64,1024]{1,0:T(8,128)S(1)}, f32[64,1024]{1,0:T(8,128)}, u32[]{:S(2)}) copy-start(f32[64,1024]{1,0:T(8,128)} %get-tuple-element.18.refs_8_.refs_0_) | copy-start | bytes 786436
  32.9 24.6 %all-to-all-start.1 = ((f32[8,80,512]{2,1,0:T(8,128)}), f32[8,80,512]{2,1,0:T(8,128)}, u32[]{:S(2)}, u32[]{:S(2)}) async-start(f32[8,80,512]{2,1,0:T(8,128)} %shard_map.86), calls=%async_computation.1 | async-start | bytes 2621440 | tf_op jit(solution)/shard_map/all_to_all | solution.py:41
  37.3 6.5 %collective-permute-start.7 = (f32[64,1024]{1,0:T(8,128)S(1)}, f32[64,1024]{1,0:T(8,128)S(1)}, u32[]{:S(2)}, u32[]{:S(2)}) collective-permute-start(f32[64,1024]{1,0:T(8,128)S(1)} %copy-done.11), channel_id=1, source_target_pairs={{0,8},{8,16},{16,24},{24,32},{32,40},{40,48},{48,56},{56,0},{1,9},... | collective-permute-start | bytes 786440 | tf_op jit(solution)/shard_map/ppermute | solution.py:53
  38.6 5.6 %collective-permute-start.10 = (f32[64,1024]{1,0:T(8,128)S(1)}, f32[64,1024]{1,0:T(8,128)S(1)}, u32[]{:S(2)}, u32[]{:S(2)}) collective-permute-start(f32[64,1024]{1,0:T(8,128)S(1)} %copy-done.11), channel_id=1, source_target_pairs={{0,56},{8,0},{16,8},{24,16},{32,24},{40,32},{48,40},{56,48},{1,57}... | collective-permute-start | bytes 786440 | tf_op jit(solution)/shard_map/ppermute | solution.py:53
  43.8 16.4 %copy-start.13 = (f32[64,1024]{1,0:T(8,128)}, f32[64,1024]{1,0:T(8,128)S(1)}, u32[]{:S(2)}) copy-start(f32[64,1024]{1,0:T(8,128)S(1)} %collective-permute-done.7.refs_9_.refs_1_) | copy-start | bytes 786436
  43.8 6.8 %collective-permute-start.8 = (f32[64,1024]{1,0:T(8,128)S(1)}, f32[64,1024]{1,0:T(8,128)S(1)}, u32[]{:S(2)}, u32[]{:S(2)}) collective-permute-start(f32[64,1024]{1,0:T(8,128)S(1)} %collective-permute-done.7.refs_9_.refs_1_), channel_id=1, source_target_pairs={{0,8},{8,16},{16,24},{24,32},{32,40},{40,48},{48,56},{56,0},{1,9},... | collective-permute-start | bytes 786440 | tf_op jit(solution)/shard_map/ppermute | solution.py:53
  44.2 16.1 %copy-start.15 = (f32[64,1024]{1,0:T(8,128)}, f32[64,1024]{1,0:T(8,128)S(1)}, u32[]{:S(2)}) copy-start(f32[64,1024]{1,0:T(8,128)S(1)} %collective-permute-done.10.refs_13_.refs_5_) | copy-start | bytes 786436
  44.2 6.8 %collective-permute-start.11 = (f32[64,1024]{1,0:T(8,128)S(1)}, f32[64,1024]{1,0:T(8,128)S(1)}, u32[]{:S(2)}, u32[]{:S(2)}) collective-permute-start(f32[64,1024]{1,0:T(8,128)S(1)} %collective-permute-done.10.refs_13_.refs_5_), channel_id=1, source_target_pairs={{0,56},{8,0},{16,8},{24,16},{32,24},{40,32},{48,40},{56,48},{1,57}... | collective-permute-start | bytes 786440 | tf_op jit(solution)/shard_map/ppermute | solution.py:53
  46.5 9.8 %collective-permute-start.6 = (f32[64,1024]{1,0:T(8,128)S(1)}, f32[64,1024]{1,0:T(8,128)S(1)}, u32[]{:S(2)}, u32[]{:S(2)}) collective-permute-start(f32[64,1024]{1,0:T(8,128)S(1)} %collective-permute-done.5.refs_5_.refs_7_), channel_id=1, source_target_pairs={{0,3},{1,0},{2,1},{3,2},{4,7},{5,4},{6,5},{7,6},{8,11},{9,8},{10,9... | collective-permute-start | bytes 786440 | tf_op jit(solution)/shard_map/ppermute | solution.py:37
  50.7 9.6 %copy-start.17 = (f32[64,1024]{1,0:T(8,128)}, f32[64,1024]{1,0:T(8,128)S(1)}, u32[]{:S(2)}) copy-start(f32[64,1024]{1,0:T(8,128)S(1)} %collective-permute-done.8.refs_10_.refs_2_) | copy-start | bytes 786436
  50.7 10.1 %collective-permute-start.9 = (f32[64,1024]{1,0:T(8,128)S(1)}, f32[64,1024]{1,0:T(8,128)S(1)}, u32[]{:S(2)}, u32[]{:S(2)}) collective-permute-start(f32[64,1024]{1,0:T(8,128)S(1)} %collective-permute-done.8.refs_10_.refs_2_), channel_id=1, source_target_pairs={{0,8},{8,16},{16,24},{24,32},{32,40},{40,48},{48,56},{56,0},{1,9},... | collective-permute-start | bytes 786440 | tf_op jit(solution)/shard_map/ppermute | solution.py:53
  51.0 9.3 %copy-start.19 = (f32[64,1024]{1,0:T(8,128)}, f32[64,1024]{1,0:T(8,128)S(1)}, u32[]{:S(2)}) copy-start(f32[64,1024]{1,0:T(8,128)S(1)} %collective-permute-done.11.refs_14_.refs_6_) | copy-start | bytes 786436
  51.0 11.0 %collective-permute-start.12 = (f32[64,1024]{1,0:T(8,128)S(1)}, f32[64,1024]{1,0:T(8,128)S(1)}, u32[]{:S(2)}, u32[]{:S(2)}) collective-permute-start(f32[64,1024]{1,0:T(8,128)S(1)} %collective-permute-done.11.refs_14_.refs_6_), channel_id=1, source_target_pairs={{0,56},{8,0},{16,8},{24,16},{32,24},{40,32},{48,40},{56,48},{1,57}... | collective-permute-start | bytes 786440 | tf_op jit(solution)/shard_map/ppermute | solution.py:53
  56.3 1.1 copy-start.29
  60.3 15.9 %collective-permute-start.14 = (f32[128,1536]{1,0:T(8,128)}, f32[128,1536]{1,0:T(8,128)S(1)}, u32[]{:S(2)}, u32[]{:S(2)}) collective-permute-start(f32[128,1536]{1,0:T(8,128)} %shard_map.87.refs_0_.refs_8_), channel_id=1, source_target_pairs={{0,128},{64,192},{128,0},{192,64},{1,129},{65,193},{129,1},{193,65... | collective-permute-start | bytes 2359304 | tf_op jit(solution)/shard_map/ppermute | solution.py:374
  60.8 1.2 copy-start.21
  60.8 13.6 %collective-permute-start.13 = (f32[64,1024]{1,0:T(8,128)S(1)}, f32[64,1024]{1,0:T(8,128)S(1)}, u32[]{:S(2)}, u32[]{:S(2)}) collective-permute-start(f32[64,1024]{1,0:T(8,128)S(1)} %collective-permute-done.9.refs_1_.refs_11_.refs_3_), channel_id=1, source_target_pairs={{0,8},{8,16},{16,24},{24,32},{32,40},{40,48},{48,56},{56,0},{1,9},... | collective-permute-start | bytes 786440 | tf_op jit(solution)/shard_map/ppermute | solution.py:53
  62.0 0.7 copy-start.23
  74.4 1.9 %copy-start.25 = (f32[64,1024]{1,0:T(8,128)}, f32[64,1024]{1,0:T(8,128)S(1)}, u32[]{:S(2)}) copy-start(f32[64,1024]{1,0:T(8,128)S(1)} %collective-permute-done.13.refs_12_.refs_4_) | copy-start | bytes 786436
  76.2 0.9 copy-start.9
  77.1 23.8 %copy-start.12 = (f32[64,1024]{1,0:T(8,128)S(1)}, f32[64,1024]{1,0:T(8,128)}, u32[]{:S(2)}) copy-start(f32[64,1024]{1,0:T(8,128)} %get-tuple-element.18.refs_8_.refs_0_) | copy-start | bytes 786436
  77.1 23.8 %copy-start.14 = (f32[64,1024]{1,0:T(8,128)S(1)}, f32[64,1024]{1,0:T(8,128)}, u32[]{:S(2)}) copy-start(f32[64,1024]{1,0:T(8,128)} %copy-done.13) | copy-start | bytes 786436
  77.1 23.8 %copy-start.16 = (f32[64,1024]{1,0:T(8,128)S(1)}, f32[64,1024]{1,0:T(8,128)}, u32[]{:S(2)}) copy-start(f32[64,1024]{1,0:T(8,128)} %copy-done.15) | copy-start | bytes 786436
  77.1 23.8 %copy-start.18 = (f32[64,1024]{1,0:T(8,128)S(1)}, f32[64,1024]{1,0:T(8,128)}, u32[]{:S(2)}) copy-start(f32[64,1024]{1,0:T(8,128)} %copy-done.17) | copy-start | bytes 786436
  77.1 23.8 %copy-start.20 = (f32[64,1024]{1,0:T(8,128)S(1)}, f32[64,1024]{1,0:T(8,128)}, u32[]{:S(2)}) copy-start(f32[64,1024]{1,0:T(8,128)} %copy-done.19) | copy-start | bytes 786436
  77.2 23.8 %copy-start.22 = (f32[64,1024]{1,0:T(8,128)S(1)}, f32[64,1024]{1,0:T(8,128)}, u32[]{:S(2)}) copy-start(f32[64,1024]{1,0:T(8,128)} %copy-done.21) | copy-start | bytes 786436
  77.2 23.8 %copy-start.24 = (f32[64,1024]{1,0:T(8,128)S(1)}, f32[64,1024]{1,0:T(8,128)}, u32[]{:S(2)}) copy-start(f32[64,1024]{1,0:T(8,128)} %copy-done.23) | copy-start | bytes 786436
  88.1 6.9 %collective-permute-start.18 = (f32[1024,256]{1,0:T(8,128)}, f32[1024,256]{1,0:T(8,128)S(1)}, u32[]{:S(2)}, u32[]{:S(2)}) collective-permute-start(f32[1024,256]{1,0:T(8,128)} %get-tuple-element.28), channel_id=1, source_target_pairs={{0,64},{64,0},{128,192},{192,128},{1,65},{65,1},{129,193},{193,129... | collective-permute-start | bytes 3145736 | tf_op jit(solution)/shard_map/ppermute | solution.py:400
  92.5 8.4 %collective-permute-start.17 = (f32[1024,256]{1,0:T(8,128)}, f32[1024,256]{1,0:T(8,128)S(1)}, u32[]{:S(2)}, u32[]{:S(2)}) collective-permute-start(f32[1024,256]{1,0:T(8,128)} %get-tuple-element.23), channel_id=1, source_target_pairs={{0,64},{64,0},{128,192},{192,128},{1,65},{65,1},{129,193},{193,129... | collective-permute-start | bytes 3145736 | tf_op jit(solution)/shard_map/ppermute | solution.py:401
  95.0 2.0 %copy-start.1 = (f32[128,1536]{1,0:T(8,128)S(1)}, f32[128,1536]{1,0:T(8,128)}, u32[]{:S(2)}) copy-start(f32[128,1536]{1,0:T(8,128)} %shard_map.87.refs_0_.refs_8_) | copy-start | bytes 2359300
  95.0 6.0 %copy-start = (f32[1088,272]{0,1:T(8,128)S(1)}, f32[1088,272]{0,1:T(8,128)}, u32[]{:S(2)}) copy-start(f32[1088,272]{0,1:T(8,128)} %param.8) | copy-start | bytes 3551236
  95.0 6.0 %copy-start.8 = (f32[1024,256]{1,0:T(8,128)S(1)}, f32[1024,256]{1,0:T(8,128)}, u32[]{:S(2)}) copy-start(f32[1024,256]{1,0:T(8,128)} %get-tuple-element.24.refs_13_) | copy-start | bytes 3145732
  95.0 6.0 %copy-start.27 = (s32[3]{0:T(128)S(1)}, s32[3]{0:T(128)}, u32[]{:S(2)}) copy-start(s32[3]{0:T(128)} %pad_add_fusion.meta) | copy-start | bytes 40
  95.0 6.0 %copy-start.28 = (s32[512]{0:T(512)S(1)}, s32[512]{0:T(512)}, u32[]{:S(2)}) copy-start(s32[512]{0:T(512)} %param.9) | copy-start | bytes 6148
  96.5 24.5 %collective-permute-start.19 = (f32[1024,256]{1,0:T(8,128)S(1)}, f32[1024,256]{1,0:T(8,128)S(1)}, u32[]{:S(2)}, u32[]{:S(2)}) collective-permute-start(f32[1024,256]{1,0:T(8,128)S(1)} %add.6), channel_id=1, source_target_pairs={{0,128},{64,192},{128,0},{192,64},{1,129},{65,193},{129,1},{193,65... | collective-permute-start | bytes 3145736 | tf_op jit(solution)/shard_map/ppermute | solution.py:402
  97.0 3.7 %collective-permute-start.15 = (f32[128,1536]{1,0:T(8,128)S(1)}, f32[128,1536]{1,0:T(8,128)S(1)}, u32[]{:S(2)}, u32[]{:S(2)}) collective-permute-start(f32[128,1536]{1,0:T(8,128)S(1)} %copy-done.1), channel_id=1, source_target_pairs={{0,64},{64,0},{128,192},{192,128},{1,65},{65,1},{129,193},{193,129... | collective-permute-start | bytes 2359304 | tf_op jit(solution)/shard_map/ppermute | solution.py:404
  97.7 3.2 %collective-permute-start.16 = (f32[128,1536]{1,0:T(8,128)}, f32[128,1536]{1,0:T(8,128)S(1)}, u32[]{:S(2)}, u32[]{:S(2)}) collective-permute-start(f32[128,1536]{1,0:T(8,128)} %copy-done.9), channel_id=1, source_target_pairs={{0,64},{64,0},{128,192},{192,128},{1,65},{65,1},{129,193},{193,129... | collective-permute-start | bytes 2359304 | tf_op jit(solution)/shard_map/ppermute | solution.py:404
  101.0 1.1 copy-start.10
  102.2 0.9 copy-start.26
